TPU v7x, 256 devices: a whole 4x4x8 slice. The times are simulated.
256 devices in a mesh: batch: 2 (over x_hi), seq: 8 (over z), pool: 16 (over y, x_lo, core).
Axes of the slice: x: 4 (x_hi: 2, x_lo: 2; x = x_hi * 2 + x_lo), y: 4, z: 8, core: 2. Of those that a mesh axis runs over, the one named last changes fastest.
Arguments:
- tokens: bfloat16 [32, 2048, 1024], P(('batch', 'pool'), 'seq'), may hold values from -6 to 6
- w_in: bfloat16 [1024, 4096], replicated, may hold values from -0.1875 to 0.1875
- w_out: bfloat16 [1024, 1024], replicated, may hold values from -0.1875 to 0.1875
- w_proj: bfloat16 [1024, 256], replicated, may hold values from -0.1875 to 0.1875
- pos_embed: bfloat16 [32, 2048, 256], P(('batch', 'pool'), 'seq'), may hold values from -6 to 6
- pos_ids: int32 [32, 2048], P(('batch', 'pool'), 'seq'), may hold values from 0 to 1048575
- lengths: int32 [32], P(('batch', 'pool')), may hold values from 256 to 2048, as said below
- neg_embed: bfloat16 [2, 4096, 256], P('batch', 'pool'), may hold values from -0.375 to 0.375
- neg_ids: int32 [2, 4096], P('batch', 'pool'), may hold values from 0 to 1048575
Outputs:
- loss: float32 [32, 2048], P(('batch', 'pool'), 'seq')
- d_neg: float32 [2, 4096, 256], P('batch', 'pool', 'seq')
- d_proj: float32 [1024, 256], replicated
Inputs may be any that keep to these rules, and one draw needn't show every extreme that they name: `lengths`: every history has at least one valid event; in every draw one history is valid over all 2048 events.
All inputs are finite; a program needn't handle non-finite values.
Results may differ from a plain program's by a relative error of at most 0.017.
Values may be sent and summed in bfloat16 or wider, within the bound.
A program may use at most 128 MiB of HBM per device.

v0:
```python
import math

import jax
import jax.numpy as jnp
from jax import lax
from jax.sharding import PartitionSpec as P

HEADS = 8
ITEMS = 1048576


SOFTMAX_WARMTH = 0.02
NORM_EPSILON = 1e-05
UNIT_EPSILON = 1e-06


def layer_norm(inputs):
    center = inputs - jnp.mean(inputs, axis=-1, keepdims=True)
    spread = jnp.mean(center * center, axis=-1, keepdims=True)
    return center / jnp.sqrt(spread + NORM_EPSILON)


def unit_rows(inputs):
    norms = jnp.sqrt(jnp.sum(inputs * inputs, axis=-1, keepdims=True) + UNIT_EPSILON)
    return (inputs / norms, norms)


def log_sample_chance(item_ids):
    ranks = item_ids.astype(jnp.float32) + 1.0
    return jnp.log(jnp.log1p(1.0 / ranks)) - jnp.log(jnp.log(jnp.float32(ITEMS) + 1.0))


def head_split(block):
    return block.reshape(block.shape[0], HEADS, block.shape[1] // HEADS).transpose(1, 0, 2)


def attend(query_block, query_pos, key_block, value_block, key_pos, length):
    width = query_block.shape[1]
    head_width = width // HEADS
    allowed = (key_pos[None, :] <= query_pos[:, None]) & (key_pos[None, :] < length)

    def one_head(parts):
        query_head, key_head, value_head = parts
        scores = jnp.dot(query_head, key_head.T, preferred_element_type=jnp.float32) / math.sqrt(
            head_width
        )
        weights = jnp.where(allowed, jax.nn.silu(scores), 0.0).astype(jnp.bfloat16)
        return jnp.dot(weights, value_head, preferred_element_type=jnp.float32)

    result = lax.map(
        one_head, (head_split(query_block), head_split(key_block), head_split(value_block))
    )
    return result.transpose(1, 0, 2).reshape(query_block.shape[0], width)


def body(tokens, w_in, w_out, w_proj, pos_embed, pos_ids, lengths, neg_embed, neg_ids):
    rows = tokens.shape[1]
    width = tokens.shape[2]
    seq_count = lax.axis_size("seq")
    pool_count = lax.axis_size("pool")
    hist_count = lax.axis_size("batch") * pool_count
    first = lax.axis_index("seq") * rows
    length = lengths[0]
    history = tokens[0]
    own_pos = first + jnp.arange(rows, dtype=jnp.int32)
    normed = layer_norm(history.astype(jnp.float32)).astype(jnp.bfloat16)
    mixed = jax.nn.silu(jnp.dot(normed, w_in, preferred_element_type=jnp.float32))
    gate_u = mixed[:, :width].astype(jnp.bfloat16)
    values = mixed[:, width : 2 * width].astype(jnp.bfloat16)
    queries = mixed[:, 2 * width : 3 * width].astype(jnp.bfloat16)
    keys = mixed[:, 3 * width :].astype(jnp.bfloat16)
    key_block = lax.all_gather(keys, "seq", axis=0, tiled=True)
    value_block = lax.all_gather(values, "seq", axis=0, tiled=True)
    key_pos = jnp.arange(key_block.shape[0], dtype=jnp.int32)
    attn = attend(queries, own_pos, key_block, value_block, key_pos, length)
    gated = (layer_norm(attn) * gate_u.astype(jnp.float32)).astype(jnp.bfloat16)
    layer_out = (
        jnp.dot(gated, w_out, preferred_element_type=jnp.float32) + history.astype(jnp.float32)
    ).astype(jnp.bfloat16)
    out_unit, out_norms = unit_rows(jnp.dot(layer_out, w_proj, preferred_element_type=jnp.float32))
    output_estimate = out_unit.astype(jnp.bfloat16)
    positive_direction = unit_rows(pos_embed[0].astype(jnp.float32))[0]
    positive_targets = pos_ids[0]
    valid = own_pos < length
    positive_score = jnp.sum(
        output_estimate.astype(jnp.float32) * positive_direction, axis=-1
    ) / SOFTMAX_WARMTH - log_sample_chance(positive_targets)
    embed_width = output_estimate.shape[1]
    col_width = embed_width // seq_count
    table, table_ids = (
        lax.all_gather(neg_embed[0], "pool", axis=0, tiled=True),
        lax.all_gather(neg_ids[0], "pool", axis=0, tiled=True),
    )
    unit_negs, neg_norms = unit_rows(table.astype(jnp.float32))
    negative_estimate = unit_negs.astype(jnp.bfloat16)
    negative_score = (
        jnp.dot(output_estimate, negative_estimate.T, preferred_element_type=jnp.float32)
        / SOFTMAX_WARMTH
        - log_sample_chance(table_ids)[None, :]
    )
    kept = jnp.where(table_ids[None, :] != positive_targets[:, None], jnp.exp(negative_score), 0.0)
    total = jnp.exp(positive_score) + jnp.sum(kept, axis=-1)
    negative_weights = (jnp.where(valid[:, None], kept / total[:, None], 0.0) / hist_count).astype(
        jnp.bfloat16
    )
    negative_portion = (
        jnp.dot(negative_weights.T, output_estimate, preferred_element_type=jnp.float32)
        / SOFTMAX_WARMTH
    )
    neg_term = (
        negative_portion - unit_negs * jnp.sum(unit_negs * negative_portion, axis=-1, keepdims=True)
    ) / neg_norms
    shard_rows = neg_term.shape[0] // pool_count
    blocks = neg_term.reshape(pool_count, shard_rows, seq_count, col_width).transpose(2, 0, 1, 3)
    blocks = blocks.reshape(seq_count * pool_count, shard_rows, col_width)
    d_neg = lax.psum_scatter(blocks, ("seq", "pool"), scatter_dimension=0, tiled=True)
    negative_rows = jnp.dot(negative_weights, negative_estimate, preferred_element_type=jnp.float32)
    loss = jnp.where(valid, jnp.log(total) - positive_score, 0.0)
    positive_weight = jnp.where(valid, jnp.exp(positive_score) / total - 1.0, 0.0) / hist_count
    unit_gradient = (positive_weight[:, None] * positive_direction + negative_rows) / SOFTMAX_WARMTH
    d_out = (
        (unit_gradient - out_unit * jnp.sum(out_unit * unit_gradient, axis=-1, keepdims=True))
        / out_norms
    ).astype(jnp.bfloat16)
    proj_term = jnp.dot(layer_out.T, d_out, preferred_element_type=jnp.float32)
    d_proj = lax.psum(proj_term, ("batch", "seq", "pool"))
    return (loss[None, :], d_neg, d_proj)


def solution(mesh):
    placed = (
        P(("batch", "pool"), "seq", None),
        P(),
        P(),
        P(),
        P(("batch", "pool"), "seq", None),
        P(("batch", "pool"), "seq"),
        P(("batch", "pool")),
        P("batch", "pool", None),
        P("batch", "pool"),
    )
    return jax.shard_map(
        body,
        mesh=mesh,
        in_specs=placed,
        out_specs=(P(("batch", "pool"), "seq"), P("batch", "pool", "seq"), P()),
        check_vma=False,
    )
```

profile of v0, /device:TPU:1, one launch (start us, length us, event | category | flops | bytes accessed | tf_op | source)
XLA Modules:
  0.0 1027.6 jit_solution(5778946801993316832)
XLA Ops:
  7.2 1.8 copy.17
  9.1 0.0 all-gather.8.cloned.1.call-start
  9.1 1.2 convert_reduce_fusion
  10.3 1.3 fusion.36
  11.6 6.1 multiply_convert_fusion.1
  17.8 1.3 copy-done.4
  19.1 1.2 fusion.61
  20.3 0.0 all-gather.6.cloned.1.call-start
  20.4 0.7 all-gather.6.cloned.1.call-update
  21.0 0.0 all-reduce.2.cloned.1.call-start
  21.1 1.9 copy.29
  23.7 0.1 copy.16
  23.8 21.2 %all-gather = s32[1,4096]{1,0:T(1,128)S(1)} all-gather(s32[1,256]{1,0:T(1,128)S(1)} %copy-done.8), channel_id=2, replica_groups=mesh['batch'=2,'seq'=8,'pool'=16] {'pool'}, dimensions={1}, use_global_device_ids=true | all-gather | bytes 17408 | tf_op jit(solution)/shard_map/all_gather | solution.py:92
  45.1 0.1 fusion.53
  45.2 8.7 all-gather.10.cloned.1.call-done
  53.9 2.0 fusion.29
  55.9 55.0 %all-gather.8.cloned.1.call-done = bf16[2048,1024]{1,0:T(8,128)(2,1)} async-done(((bf16[256,1024]{1,0:T(8,128)(2,1)}), bf16[2048,1024]{1,0:T(8,128)(2,1)}) %all-gather.8.cloned.1.call-update) | async-done | bytes 4194320 | tf_op jit(solution)/shard_map/all_gather | solution.py:73
  110.9 4.9 bitcast_bitcast_fusion
  115.9 50.3 %all-gather.6.cloned.1.call-done = bf16[2048,1024]{1,0:T(8,128)(2,1)} async-done(((bf16[256,1024]{1,0:T(8,128)(2,1)}), bf16[2048,1024]{1,0:T(8,128)(2,1)}) %all-gather.6.cloned.1.call-update) | async-done | bytes 4194320 | tf_op jit(solution)/shard_map/all_gather | solution.py:72
  166.2 4.9 bitcast_bitcast_fusion.1
  171.1 20.0 %while.11 = (s32[]{:T(128)}, f32[8,256,128]{2,1,0:T(8,128)S(1)}, bf16[8,256,128]{2,1,0:T(8,128)(2,1)}, bf16[8,2048,128]{2,1,0:T(8,128)(2,1)}, bf16[8,2048,128]{2...) while((s32[]{:T(128)}, f32[8,256,128]{2,1,0:T(8,128)S(1)}, ...), condition=%wide.region_3.4_spmd.clone, body=%wide.region_2.3_spmd.clone.sunk | while | flops 273154048 | bytes 1250389 | solution.py:50
  171.1 2.5 fusion.80
  173.6 2.5 fusion.80
  176.1 2.5 fusion.80
  178.6 2.5 fusion.80
  181.1 2.5 fusion.80
  183.6 2.5 fusion.80
  186.1 2.5 fusion.80
  188.6 2.5 fusion.80
  191.1 0.1 reduce_sum.103
  191.3 0.3 fusion.42
  191.6 2.1 fusion.32
  193.7 0.4 multiply_reduce_fusion.3
  194.1 0.1 multiply_reduce_fusion.2
  194.2 1.6 fusion.62
  195.8 0.8 multiply_convert_fusion
  196.7 0.8 multiply_reduce_fusion.1
  197.4 0.6 copy-done.3
  198.0 1.3 fusion.54
  199.4 0.2 reduce-scatter.2.cloned.1.call-start
  199.6 3.4 multiply_reduce_fusion
  203.0 1.0 subtract_divide_fusion
  204.0 1.7 copy.23
  205.8 4.3 copy.18
  210.1 0.6 compare_select_fusion
  210.7 241.8 %all-reduce.2.cloned.1.call-done = f32[1024,256]{1,0:T(8,128)} async-done(((f32[1024,256]{1,0:T(8,128)}), f32[1024,256]{1,0:T(8,128)}) %all-reduce.2.cloned.1.call-update) | async-done | bytes 1048592 | tf_op jit(solution)/shard_map/psum | solution.py:126
  452.5 566.3 %reduce-scatter.2.cloned.1.call-done = f32[1,256,32]{1,2,0:T(8,128)} async-done(((f32[128,256,32]{1,2,0:T(8,128)}), f32[1,256,32]{1,2,0:T(8,128)}) %reduce-scatter.2.cloned.1.call-update) | async-done | bytes 32784 | tf_op jit(solution)/shard_map/reduce_scatter | solution.py:116
  1018.8 2.3 copy.41
  (34 shorter events, 0.3 us)
Async XLA Ops:
  7.2 184.4 %copy-start = (bf16[1024,1024]{1,0:T(8,128)(2,1)S(1)}, bf16[1024,1024]{1,0:T(8,128)(2,1)}, u32[]{:S(2)}) copy-start(bf16[1024,1024]{1,0:T(8,128)(2,1)} %param.13) | copy-start | bytes 6291460
  7.2 46.7 %all-gather.10.cloned.1.call-start = ((), (), s32[]{:S(2)}) async-start(), calls=%async_computation.5 | async-start | bytes 2228224 | tf_op jit(solution)/shard_map/all_gather | solution.py:91
  9.1 101.9 %all-gather.8.cloned.1.call-start = ((), (), s32[]{:S(2)}) async-start(), calls=%async_computation.2 | async-start | bytes 4718592 | tf_op jit(solution)/shard_map/all_gather | solution.py:73
  17.8 1.3 copy-start.4
  19.1 4.6 copy-start.6
  19.1 4.7 copy-start.8
  20.3 145.9 %all-gather.6.cloned.1.call-start = ((), (), s32[]{:S(2)}) async-start(), calls=%async_computation.1 | async-start | bytes 4718592 | tf_op jit(solution)/shard_map/all_gather | solution.py:72
  21.0 431.4 %all-reduce.2.cloned.1.call-start = ((), (), s32[]{:S(2)}) async-start(), calls=%async_computation.4 | async-start | bytes 2097152 | tf_op jit(solution)/shard_map/psum | solution.py:126
  191.5 2.2 copy-start.5
  191.6 2.6 copy-start.7
  191.6 2.6 copy-start.1
  196.6 1.4 copy-start.3
  199.4 819.5 %reduce-scatter.2.cloned.1.call-start = ((), (), s32[]{:S(2)}) async-start(), calls=%async_computation.3 | async-start | bytes 4227072 | tf_op jit(solution)/shard_map/reduce_scatter | solution.py:116
  199.6 3.4 copy-start.2
Sparse Core Ops, SparseCore 0:
  9.8 44.0 all-gather.9
  56.3 54.6 all-gather.7
  112.7 53.4 all-gather.5
  199.5 252.9 all-reduce.1
  455.6 563.2 reduce-scatter.1
where the time goes:
time: 1030 us
  waiting for transfers between devices  923 us (90%)
  matrix products  35.5 us (3%)
  local copies, waits for them, and re-layouts  25.1 us (2%)
  blocking collectives  21.2 us (2%)
  between operations  14.7 us (1%)
    reduce_scatter x1, waiting for transfers between devices, body(): lax.psum_scatter(blocks, ('seq', 'pool'), scatter_dimension=0, tiled=True)  566 us
    psum x1, waiting for transfers between devices, body(): d_proj = lax.psum(proj_term, ('batch', 'seq', 'pool'))  242 us
    all_gather x1, waiting for transfers between devices, body(): value_block = lax.all_gather(values, 'seq', axis=0, tiled=True)  55 us
    all_gather x1, waiting for transfers between devices, body(): key_block = lax.all_gather(keys, 'seq', axis=0, tiled=True)  50.3 us
    all_gather x1, blocking collectives, body(): lax.all_gather(neg_ids[0], 'pool', axis=0, tiled=True)  21.2 us
  transfers between devices with their start and end apart: 5, of which 5 were waited for; matrix products, arithmetic and copies ran while one was open for 3% of the time, Pallas kernels for 0%

commit v1 on v0

v1 whole, which is shorter than its diff:
```python
import math

import jax
import jax.numpy as jnp
from jax import lax
from jax.experimental import pallas as pl
from jax.experimental.pallas import tpu as pltpu
from jax.sharding import PartitionSpec as P

HEADS = 8
HEAD = 128
ROWS = 256
WIDTH = 1024
EMBED = 256
SEQ = 8
POOL = 16
BATCH = 2
GRID = 16
ITEMS = 1048576
HIST = 32
WARMTH = 0.02
NORM_EPSILON = 1e-05
UNIT_EPSILON = 1e-06
MESH = pl.DeviceIdType.MESH
F32 = jnp.float32
BF16 = jnp.bfloat16


def dot(a, b):
    return jnp.dot(a, b, preferred_element_type=F32)


def dot_nt(a, b):
    return lax.dot_general(a, b, (((1,), (1,)), ((), ())), preferred_element_type=F32)


def dot_tn(a, b):
    return lax.dot_general(a, b, (((0,), (0,)), ((), ())), preferred_element_type=F32)


def silu(v):
    half = 0.5 * v
    return half + half * jnp.tanh(half)


def layer_norm(inputs):
    center = inputs - jnp.mean(inputs, axis=-1, keepdims=True)
    spread = jnp.mean(center * center, axis=-1, keepdims=True)
    return center * lax.rsqrt(spread + NORM_EPSILON)


def inverse_chance(ids):
    z = 1.0 / (2.0 * ids + 3.0)
    z2 = z * z
    series = 1.0 / 17.0
    for odd in (15, 13, 11, 9, 7, 5, 3, 1):
        series = series * z2 + 1.0 / odd
    return math.log(ITEMS + 1.0) / (2.0 * z * series)


def far_first(i):
    return 4 + (1 - 2 * (i % 2)) * ((i + 1) // 2)


def remote(src, dst, send, recv, **device):
    return pltpu.make_async_remote_copy(
        src_ref=src, dst_ref=dst, send_sem=send, recv_sem=recv, device_id=device, device_id_type=MESH
    )


def kernel(
    tokens,
    w_in,
    w_out,
    w_proj,
    pos_embed,
    pos_ids,
    lengths,
    neg_embed,
    neg_ids,
    loss_ref,
    dneg_ref,
    dproj_ref,
    wkv,
    wq,
    wg,
    wo,
    wp,
    normed,
    kvs,
    kvr,
    qs,
    qr,
    osend,
    orecv,
    gate,
    negs,
    negs_t,
    ids_all,
    cmask,
    kept,
    pos_t,
    cs,
    cr,
    own,
    xs,
    xr,
    ys,
    yr,
    zs,
    zr,
    pcs,
    pcr,
    pown,
    pzs,
    pzr,
    pxr,
    fin,
    w_sem,
    kv_sem,
    q_sem,
    o_sem,
    neg_sem,
    id_sem,
    c_sem,
    x_sem,
    y_sem,
    z_sem,
    pc_sem,
    pz_sem,
    px_sem,
    f_sem,
    fc_sem,
):
    b = lax.axis_index("batch")
    s = lax.axis_index("seq")
    p = lax.axis_index("pool")
    core = p % 2
    xlo = (p // 2) % 2
    y = p // 4
    sibling = p + 1 - 2 * core
    across = p + 2 - 4 * xlo
    q_own = b * 8 + p // 2

    def load_kv(k):
        h = (s + k) % SEQ
        return [
            pltpu.make_async_copy(
                w_in.at[:, pl.ds(pl.multiple_of(3 * WIDTH + h * HEAD, HEAD), HEAD)],
                wkv.at[k, :, pl.ds(0, HEAD)],
                w_sem.at[k],
            ),
            pltpu.make_async_copy(
                w_in.at[:, pl.ds(pl.multiple_of(WIDTH + h * HEAD, HEAD), HEAD)],
                wkv.at[k, :, pl.ds(HEAD, HEAD)],
                w_sem.at[8 + k],
            ),
        ]

    def load_q(i, half):
        h = (s + far_first(2 * i + half)) % SEQ
        return pltpu.make_async_copy(
            w_in.at[:, pl.ds(pl.multiple_of(2 * WIDTH + h * HEAD, HEAD), HEAD)],
            wq.at[i, :, pl.ds(half * HEAD, HEAD)],
            w_sem.at[16 + 2 * i + half],
        )

    load_g = pltpu.make_async_copy(w_in.at[:, pl.ds(0, WIDTH)], wg, w_sem.at[24])
    load_o = pltpu.make_async_copy(w_out, wo, w_sem.at[25])
    load_p = pltpu.make_async_copy(w_proj, wp, w_sem.at[26])
    for i in range(8):
        for c in load_kv(far_first(i)):
            c.start()
    for i in range(4):
        load_q(i, 0).start()
        load_q(i, 1).start()
    load_g.start()
    load_o.start()
    load_p.start()

    barrier = pltpu.get_barrier_semaphore()

    @pl.loop(1, SEQ)
    def _(k):
        pl.semaphore_signal(barrier, inc=1, device_id={"seq": (s + k) % SEQ}, device_id_type=MESH)

    @pl.loop(1, POOL)
    def _(k):
        pl.semaphore_signal(barrier, inc=1, device_id={"pool": (p + k) % POOL}, device_id_type=MESH)

    @pl.loop(0, POOL // 2)
    def _(k):
        pl.semaphore_signal(
            barrier, inc=1, device_id={"batch": 1 - b, "pool": 2 * k + core}, device_id_type=MESH
        )

    @pl.loop(0, 4)
    def _(i):
        rows = pl.ds(pl.multiple_of(i * 64, 64), 64)
        normed[rows, :] = layer_norm(tokens[rows, :].astype(F32)).astype(BF16)

    length = lengths[0]
    row_pos = s * ROWS + lax.broadcasted_iota(jnp.int32, (ROWS, 1), 0)
    row_valid = row_pos < length

    pl.semaphore_wait(barrier, (SEQ - 1) + (POOL - 1) + POOL // 2)

    def send_kv(k):
        return remote(
            kvs.at[k], kvr.at[s], kv_sem.at[0, k], kv_sem.at[1, k], seq=(s + k) % SEQ
        )

    def recv_kv(k):
        return remote(
            kvs.at[k], kvr.at[(s + SEQ - k) % SEQ], kv_sem.at[0, k], kv_sem.at[1, k], seq=(s + k) % SEQ
        )

    @pl.loop(0, SEQ)
    def _(i):
        k = far_first(i)
        for c in load_kv(k):
            c.wait()
        both = silu(dot(normed[...], wkv[k]))
        keys = both[:, :HEAD].astype(BF16)
        values = jnp.where(row_valid, both[:, HEAD:], 0.0).astype(BF16)

        @pl.when(i < SEQ - 1)
        def _():
            kvs[k, 0] = keys
            kvs[k, 1] = values
            send_kv(k).start()

        @pl.when(i == SEQ - 1)
        def _():
            kvr[s, 0] = keys
            kvr[s, 1] = values

    def send_q(k):
        return remote(qs.at[k], qr.at[s], q_sem.at[0, k], q_sem.at[1, k], seq=(s + k) % SEQ)

    def recv_q(k):
        return remote(
            qs.at[k], qr.at[(s + SEQ - k) % SEQ], q_sem.at[0, k], q_sem.at[1, k], seq=(s + k) % SEQ
        )

    @pl.loop(0, SEQ // 2)
    def _(i):
        load_q(i, 0).wait()
        load_q(i, 1).wait()
        both = silu(dot(normed[...], wq[i])).astype(BF16)
        k0 = far_first(2 * i)
        k1 = far_first(2 * i + 1)
        qs[k0] = both[:, :HEAD]
        send_q(k0).start()

        @pl.when(i < SEQ // 2 - 1)
        def _():
            qs[k1] = both[:, HEAD:]
            send_q(k1).start()

        @pl.when(i == SEQ // 2 - 1)
        def _():
            qr[s] = both[:, HEAD:]

    neg = neg_embed[...].astype(F32)
    neg_norm = jnp.sqrt(jnp.sum(neg * neg, axis=-1, keepdims=True) + UNIT_EPSILON)
    negs[p] = (neg / neg_norm).astype(BF16)
    ids_all[p] = neg_ids[...]

    def send_ids(k):
        return remote(ids_all.at[p], ids_all.at[p], id_sem.at[0, k], id_sem.at[1, k], pool=(p + k) % POOL)

    def recv_ids(k):
        src = (p + POOL - k) % POOL
        return remote(ids_all.at[src], ids_all.at[src], id_sem.at[0, k], id_sem.at[1, k], pool=src)

    def send_negs(k):
        return remote(negs.at[p], negs.at[p], neg_sem.at[0, k], neg_sem.at[1, k], pool=(p + k) % POOL)

    def recv_negs(k):
        src = (p + POOL - k) % POOL
        return remote(negs.at[src], negs.at[src], neg_sem.at[0, k], neg_sem.at[1, k], pool=src)

    @pl.loop(1, POOL)
    def _(k):
        send_ids(k).start()

    @pl.loop(1, POOL)
    def _(k):
        send_negs(k).start()

    load_g.wait()

    @pl.loop(0, 4)
    def _(i):
        cols = pl.ds(pl.multiple_of(i * 256, 256), 256)
        gate[:, cols] = silu(dot(normed[...], wg[:, cols])).astype(BF16)

    pos = jnp.transpose(pos_embed[...].astype(F32))
    pos_t[...] = pos / jnp.sqrt(jnp.sum(pos * pos, axis=0, keepdims=True) + UNIT_EPSILON)
    pos_row = pos_ids[...]

    @pl.loop(1, POOL)
    def _(k):
        recv_ids(k).wait_recv()

    ids = jnp.concatenate([ids_all[j] for j in range(POOL)], axis=0)
    factor = jnp.transpose(inverse_chance(ids.astype(F32)))
    ids_col = jnp.transpose(ids.astype(F32)).astype(jnp.int32)
    for j in range(POOL):
        cmask[j] = jnp.where(ids_col[:, j : j + 1] != pos_row, factor[:, j : j + 1], 0.0)

    def send_o(k):
        dst = (s + SEQ - k) % SEQ
        return remote(osend.at[k], orecv.at[s], o_sem.at[0, k], o_sem.at[1, k], seq=dst)

    def recv_o(k):
        src = (s + k) % SEQ
        return remote(osend.at[k], orecv.at[src], o_sem.at[0, k], o_sem.at[1, k], seq=src)

    @pl.loop(1, SEQ)
    def _(k):
        recv_kv(k).wait_recv()

    scale = 0.5 / math.sqrt(HEAD)

    @pl.loop(0, SEQ)
    def _(i):
        k = far_first((i + SEQ - 1) % SEQ)
        a = (s + SEQ - k) % SEQ

        @pl.when(i > 0)
        def _():
            recv_q(k).wait_recv()

        query = qr[a]

        def weights(u):
            half = scale * dot_nt(query, kvr[u, 0])
            return half + half * jnp.tanh(half)

        def group(g, total):
            return (
                total
                + dot(weights(2 * g).astype(BF16), kvr[2 * g, 1])
                + dot(weights(2 * g + 1).astype(BF16), kvr[2 * g + 1, 1])
            )

        total = lax.fori_loop(0, a // 2, group, jnp.zeros((ROWS, HEAD), F32))
        last = 2 * (a // 2)
        t_pos = a * ROWS + lax.broadcasted_iota(jnp.int32, (ROWS, ROWS), 0)
        u_pos = lax.broadcasted_iota(jnp.int32, (ROWS, ROWS), 1)
        for u in (last, last + 1):
            seen = jnp.where(u * ROWS + u_pos <= t_pos, weights(u), 0.0).astype(BF16)
            total = total + dot(seen, kvr[u, 1])

        @pl.when(i > 0)
        def _():
            osend[k] = total.astype(BF16)
            send_o(k).start()

        @pl.when(i == 0)
        def _():
            orecv[s] = total.astype(BF16)

    @pl.loop(0, POOL)
    def _(k):
        @pl.when(k > 0)
        def _():
            recv_negs(k).wait_recv()

        src = (p + POOL - k) % POOL
        negs_t[src] = jnp.transpose(negs[src])

    load_o.wait()
    load_p.wait()

    @pl.loop(1, SEQ)
    def _(k):
        recv_o(k).wait_recv()

    attn = jnp.concatenate([orecv[h] for h in range(HEADS)], axis=1).astype(F32)
    gated = (layer_norm(attn) * gate[...].astype(F32)).astype(BF16)
    layer_out = (dot(gated, wo[...]) + tokens[...].astype(F32)).astype(BF16)
    out = dot(layer_out, wp[...])
    out_hat = (out * lax.rsqrt(jnp.sum(out * out, axis=-1, keepdims=True) + UNIT_EPSILON)).astype(BF16)
    out_t = jnp.transpose(out)
    norm_t = jnp.sqrt(jnp.sum(out_t * out_t, axis=0, keepdims=True) + UNIT_EPSILON)
    unit_t = out_t / norm_t
    hat_t = unit_t.astype(BF16)
    pos_dot = jnp.sum(hat_t.astype(F32) * pos_t[...], axis=0, keepdims=True) * (1.0 / WARMTH)
    pos_chance = inverse_chance(pos_row.astype(F32))
    pos_logit = pos_dot + jnp.log(pos_chance)
    pos_exp = jnp.exp(pos_logit)

    def scores(j, total):
        value = jnp.exp(dot(negs[j], hat_t) * (1.0 / WARMTH)) * cmask[j]
        kept[j] = value
        return total + jnp.sum(value, axis=0, keepdims=True)

    total = lax.fori_loop(0, POOL, scores, jnp.zeros((1, ROWS), F32)) + pos_exp
    valid = s * ROWS + lax.broadcasted_iota(jnp.int32, (1, ROWS), 1) < length
    loss_ref[...] = jnp.where(valid, jnp.log(total) - pos_logit, 0.0)
    share = jnp.where(valid, 1.0 / (total * HIST), 0.0)
    pos_weight = jnp.where(valid, pos_exp / total - 1.0, 0.0) * (1.0 / HIST)

    def send_c(m):
        return remote(cs.at[m], cr.at[m], c_sem.at[0, m], c_sem.at[1, m], pool=sibling)

    def other_core(m, rows_t):
        j = 2 * m + 1 - core
        weight = (kept[j] * share).astype(BF16)
        cs[m] = (dot(weight, out_hat) * (1.0 / WARMTH)).astype(BF16)
        send_c(m).start()
        return rows_t + dot(negs_t[j], weight)

    def this_core(m, rows_t):
        j = 2 * m + core
        weight = (kept[j] * share).astype(BF16)
        own[m] = dot(weight, out_hat) * (1.0 / WARMTH)
        return rows_t + dot(negs_t[j], weight)

    rows_t = lax.fori_loop(0, 8, other_core, jnp.zeros((EMBED, ROWS), F32))
    rows_t = lax.fori_loop(0, 8, this_core, rows_t)

    grad_t = (pos_weight * pos_t[...] + rows_t) * (1.0 / WARMTH)
    d_out = jnp.transpose(
        (grad_t - unit_t * jnp.sum(unit_t * grad_t, axis=0, keepdims=True)) / norm_t
    ).astype(BF16)
    term = dot_tn(layer_out, d_out)
    half_rows = WIDTH // 2

    for c in range(2):
        part = term[c * half_rows : (c + 1) * half_rows]

        @pl.when(core == c)
        def _():
            pown[...] = part

        @pl.when(core != c)
        def _():
            pcs[...] = part.astype(BF16)

    send_pc = remote(pcs, pcr, pc_sem.at[0], pc_sem.at[1], pool=sibling)
    send_pc.start()

    def send_x(i):
        return remote(xs.at[i], xr.at[i], x_sem.at[0, i], x_sem.at[1, i], pool=across)

    @pl.loop(0, 4)
    def _(i):
        m = 2 * i + 1 - xlo
        send_c(m).wait_recv()
        xs[i] = (own[m] + cr[m].astype(F32)).astype(BF16)
        send_x(i).start()

    def send_pz(k):
        return remote(
            pzs.at[k], pzr.at[k], pz_sem.at[0, k], pz_sem.at[1, k], seq=(s + k) % SEQ
        )

    send_pc.wait_recv()

    @pl.loop(1, SEQ)
    def _(k):
        rows = pl.ds(pl.multiple_of(((s + k) % SEQ) * 64, 64), 64)
        pzs[k] = (pown[rows, :] + pcr[rows, :].astype(F32)).astype(BF16)
        send_pz(k).start()

    own_rows = pl.ds(pl.multiple_of(s * 64, 64), 64)
    block = pown[own_rows, :] + pcr[own_rows, :].astype(F32)

    def send_y(k):
        return remote(
            ys.at[k], yr.at[k], y_sem.at[0, k], y_sem.at[1, k], pool=((y + k) % 4) * 4 + p % 4
        )

    @pl.loop(0, 4)
    def _(i):
        m = 2 * i + xlo
        send_c(m).wait_recv()
        own[m] = own[m] + cr[m].astype(F32)

    @pl.loop(1, 4)
    def _(k):
        i = (y + k) % 4
        m = 2 * i + xlo
        send_x(i).wait_recv()
        ys[k] = (own[m] + xr[i].astype(F32)).astype(BF16)
        send_y(k).start()

    send_x(y).wait_recv()
    neg_sum = own[2 * y + xlo] + xr[y].astype(F32)

    def send_px(k):
        q = (q_own + k) % GRID
        return remote(
            pxr.at[q_own],
            pxr.at[q_own],
            px_sem.at[0, k],
            px_sem.at[1, k],
            batch=q // 8,
            pool=2 * (q % 8) + core,
        )

    def recv_px(k):
        q = (q_own + GRID - k) % GRID
        return remote(
            pxr.at[q], pxr.at[q], px_sem.at[0, k], px_sem.at[1, k], batch=q // 8, pool=2 * (q % 8) + core
        )

    for k in range(1, SEQ):
        send_pz(k).wait_recv()
        block = block + pzr[k].astype(F32)
    pxr[q_own] = block.astype(BF16)

    @pl.loop(1, GRID)
    def _(k):
        send_px(k).start()

    def send_z(k):
        return remote(zs.at[k], zr.at[k], z_sem.at[0, k], z_sem.at[1, k], seq=(s + k) % SEQ)

    for k in range(1, 4):
        send_y(k).wait_recv()
        neg_sum = neg_sum + yr[k].astype(F32)
    neg = neg_embed[...].astype(F32)
    neg_norm = jnp.sqrt(jnp.sum(neg * neg, axis=-1, keepdims=True) + UNIT_EPSILON)
    neg_unit = neg / neg_norm
    neg_term = (neg_sum - neg_unit * jnp.sum(neg_unit * neg_sum, axis=-1, keepdims=True)) / neg_norm
    cr_t = jnp.transpose(neg_term)
    own[0] = cr_t

    @pl.loop(1, SEQ)
    def _(k):
        rows = pl.ds(pl.multiple_of(((s + k) % SEQ) * 32, 32), 32)
        zs[k] = own[0, rows, :].astype(BF16)
        send_z(k).start()

    @pl.loop(1, GRID)
    def _(k):
        recv_px(k).wait_recv()

    whole = pxr[0].astype(F32)
    for q in range(1, GRID):
        whole = whole + pxr[q].astype(F32)
    fin[core * SEQ + s] = whole.astype(BF16)

    def send_f(k):
        at = core * SEQ + s
        return remote(fin.at[at], fin.at[at], f_sem.at[0, k], f_sem.at[1, k], seq=(s + k) % SEQ)

    def recv_f(k):
        at = core * SEQ + (s + SEQ - k) % SEQ
        return remote(fin.at[at], fin.at[at], f_sem.at[0, k], f_sem.at[1, k], seq=(s + k) % SEQ)

    def send_fc(k):
        at = core * SEQ + (s + SEQ - k) % SEQ
        return remote(fin.at[at], fin.at[at], fc_sem.at[0, k], fc_sem.at[1, k], pool=sibling)

    def recv_fc(k):
        at = (1 - core) * SEQ + (s + SEQ - k) % SEQ
        return remote(fin.at[at], fin.at[at], fc_sem.at[0, k], fc_sem.at[1, k], pool=sibling)

    @pl.loop(1, SEQ)
    def _(k):
        send_f(k).start()

    send_fc(0).start()

    part = own[0, pl.ds(pl.multiple_of(s * 32, 32), 32), :]
    for k in range(1, SEQ):
        send_z(k).wait_recv()
        part = part + zr[k].astype(F32)
    dneg_ref[...] = jnp.transpose(part)

    @pl.loop(1, SEQ)
    def _(k):
        recv_f(k).wait_recv()
        send_fc(k).start()

    @pl.loop(0, SEQ)
    def _(k):
        recv_fc(k).wait_recv()

    @pl.loop(0, 16)
    def _(i):
        dproj_ref[pl.ds(pl.multiple_of(i * 64, 64), 64), :] = fin[i].astype(F32)

    @pl.loop(1, SEQ)
    def _(k):
        send_kv(k).wait_send()
        send_q(k).wait_send()
        send_o(k).wait_send()
        send_pz(k).wait_send()
        send_z(k).wait_send()
        send_f(k).wait_send()

    @pl.loop(1, POOL)
    def _(k):
        send_ids(k).wait_send()
        send_negs(k).wait_send()
        send_px(k).wait_send()

    @pl.loop(0, 8)
    def _(m):
        send_c(m).wait_send()
        send_fc(m).wait_send()

    @pl.loop(0, 4)
    def _(i):
        send_x(i).wait_send()

    @pl.loop(1, 4)
    def _(k):
        send_y(k).wait_send()

    send_pc.wait_send()


def body(tokens, w_in, w_out, w_proj, pos_embed, pos_ids, lengths, neg_embed, neg_ids):
    vmem = pl.BlockSpec(memory_space=pltpu.VMEM)
    hbm = pl.BlockSpec(memory_space=pl.ANY)
    smem = pl.BlockSpec(memory_space=pltpu.SMEM)
    dma = pltpu.SemaphoreType.DMA
    loss, d_neg, d_proj = pl.pallas_call(
        kernel,
        out_shape=(
            jax.ShapeDtypeStruct((1, ROWS), F32),
            jax.ShapeDtypeStruct((ROWS, EMBED // SEQ), F32),
            jax.ShapeDtypeStruct((WIDTH, EMBED), F32),
        ),
        in_specs=[vmem, hbm, hbm, hbm, vmem, vmem, smem, vmem, vmem],
        out_specs=(vmem, vmem, vmem),
        scratch_shapes=[
            pltpu.VMEM((8, WIDTH, 256), BF16),
            pltpu.VMEM((4, WIDTH, 256), BF16),
            pltpu.VMEM((WIDTH, WIDTH), BF16),
            pltpu.VMEM((WIDTH, WIDTH), BF16),
            pltpu.VMEM((WIDTH, EMBED), BF16),
            pltpu.VMEM((ROWS, WIDTH), BF16),
            pltpu.VMEM((SEQ, 2, ROWS, HEAD), BF16),
            pltpu.VMEM((SEQ, 2, ROWS, HEAD), BF16),
            pltpu.VMEM((SEQ, ROWS, HEAD), BF16),
            pltpu.VMEM((SEQ, ROWS, HEAD), BF16),
            pltpu.VMEM((SEQ, ROWS, HEAD), BF16),
            pltpu.VMEM((SEQ, ROWS, HEAD), BF16),
            pltpu.VMEM((ROWS, WIDTH), BF16),
            pltpu.VMEM((POOL, ROWS, EMBED), BF16),
            pltpu.VMEM((POOL, EMBED, ROWS), BF16),
            pltpu.VMEM((POOL, 1, ROWS), jnp.int32),
            pltpu.VMEM((POOL, ROWS, ROWS), F32),
            pltpu.VMEM((POOL, ROWS, ROWS), F32),
            pltpu.VMEM((EMBED, ROWS), F32),
            pltpu.VMEM((8, ROWS, EMBED), BF16),
            pltpu.VMEM((8, ROWS, EMBED), BF16),
            pltpu.VMEM((8, ROWS, EMBED), F32),
            pltpu.VMEM((4, ROWS, EMBED), BF16),
            pltpu.VMEM((4, ROWS, EMBED), BF16),
            pltpu.VMEM((4, ROWS, EMBED), BF16),
            pltpu.VMEM((4, ROWS, EMBED), BF16),
            pltpu.VMEM((SEQ, 32, ROWS), BF16),
            pltpu.VMEM((SEQ, 32, ROWS), BF16),
            pltpu.VMEM((WIDTH // 2, EMBED), BF16),
            pltpu.VMEM((WIDTH // 2, EMBED), BF16),
            pltpu.VMEM((WIDTH // 2, EMBED), F32),
            pltpu.VMEM((SEQ, 64, EMBED), BF16),
            pltpu.VMEM((SEQ, 64, EMBED), BF16),
            pltpu.VMEM((GRID, 64, EMBED), BF16),
            pltpu.VMEM((16, 64, EMBED), BF16),
            dma((27,)),
            dma((2, SEQ)),
            dma((2, SEQ)),
            dma((2, SEQ)),
            dma((2, POOL)),
            dma((2, POOL)),
            dma((2, 8)),
            dma((2, 4)),
            dma((2, 4)),
            dma((2, SEQ)),
            dma((2,)),
            dma((2, SEQ)),
            dma((2, GRID)),
            dma((2, SEQ)),
            dma((2, SEQ)),
        ],
        compiler_params=pltpu.CompilerParams(
            collective_id=0, has_side_effects=True, vmem_limit_bytes=56 * 1024 * 1024
        ),
    )(
        tokens[0],
        w_in,
        w_out,
        w_proj,
        pos_embed[0],
        pos_ids,
        lengths,
        neg_embed[0],
        neg_ids,
    )
    return (loss, d_neg[None], d_proj)


def solution(mesh):
    placed = (
        P(("batch", "pool"), "seq", None),
        P(),
        P(),
        P(),
        P(("batch", "pool"), "seq", None),
        P(("batch", "pool"), "seq"),
        P(("batch", "pool")),
        P("batch", "pool", None),
        P("batch", "pool"),
    )
    return jax.shard_map(
        body,
        mesh=mesh,
        in_specs=placed,
        out_specs=(P(("batch", "pool"), "seq"), P("batch", "pool", "seq"), P()),
        check_vma=False,
    )
```

time: 1030 us -> 118 us (0.11)
  waiting for transfers between devices: 923 us -> 0 us
  Pallas kernels: 0 us -> 112 us
  matrix products: 35.5 us -> 0 us
  blocking collectives: 21.2 us -> 0 us
  local copies, waits for them, and re-layouts: 25.1 us -> 5.07 us
  between operations: 14.7 us -> 1.29 us
    reduce_scatter x1 -> x0, waiting for transfers between devices: 566 us -> none  [body(): lax.psum_scatter(blocks, ('seq', 'pool'), scatter_dimension=0, tiled=True)]
    psum x1 -> x0, waiting for transfers between devices: 242 us -> none  [body(): d_proj = lax.psum(proj_term, ('batch', 'seq', 'pool'))]
    all_gather x3 -> x0, waiting for transfers between devices: 114 us -> none  [the longest x1 55 us: body(): value_block = lax.all_gather(values, 'seq', axis=0, tiled=True)]
    pallas_call x0 -> x1, Pallas kernels: none -> 112 us  [body(): pl.pallas_call(kernel, out_shape=(jax.ShapeDtypeStruct((1, ROWS), F32), j...]
    dot_general x15 -> x0, matrix products: 35.5 us -> none  [the longest x8 19.9 us: one_head(): return jnp.dot(weights, value_head, preferred_element_type=jnp.float32)]
    all_gather x1 -> x0, blocking collectives: 21.2 us -> none  [body(): lax.all_gather(neg_ids[0], 'pool', axis=0, tiled=True)]
    transpose x3 -> x0, local copies, waits for them, and re-layouts: 14.1 us -> none  [the longest x2 9.85 us: head_split(): block.reshape(block.shape[0], HEADS, block.shape[1] // HEADS)]
  transfers between devices with their start and end apart: 5 -> 0, of which waited for: 5 -> 0; matrix products, arithmetic and copies ran while one was open for 3% -> 0% of each run, Pallas kernels for 0% -> 0%
where the time goes in v1:
time: 118 us
  Pallas kernels  112 us (95%)
  local copies, waits for them, and re-layouts  5.07 us (4%)
  between operations  1.29 us (1%)
    pallas_call x1, Pallas kernels, body(): pl.pallas_call(kernel, out_shape=(jax.ShapeDtypeStruct((1, ROWS), F32), j...  112 us
    unnamed x3, local copies, waits for them, and re-layouts  5.07 us

profile of v1, /device:TPU:1, one launch (start us, length us, event | category | flops | bytes accessed | tf_op | source)
XLA Modules:
  0.0 118.1 jit_solution(4881385637988745469)
XLA Ops:
  1.3 111.7 %shard_map.112 = (f32[1,256]{1,0:T(1,128)}, f32[256,32]{1,0:T(8,128)}, f32[1024,256]{1,0:T(8,128)}) custom-call(bf16[256,1024]{1,0:T(8,128)(2,1)} %bitcast.4, bf16[1024,4096]{1,0:T(8,128)(2,1)} %w_in.1, bf16[1024,1024]{1,0:T(8,128)(2,1)} %w_out.1, bf16[1024,256]{1,0:T(8,128)(2,1)} %w_proj.1, bf16[256,256]{1,0:T(8,128)(2,1)} %bitcast.5, s32[1,256]{1,0:T(1,128)} %pos_ids.1, ...), custom_call_target="tpu_custom_call" | custom-call | tf_op jit(solution)/shard_map/pallas_call | solution.py:626
  113.0 1.6 %copy.12 = f32[1,256,32]{1,2,0:T(8,128)} copy(f32[1,256,32]{2,1,0:T(8,128)} %bitcast.7) | data formatting | bytes 65536
  114.6 1.2 %copy.16 = f32[1,256]{1,0:T(1,128)} copy(f32[1,256]{1,0:T(1,128)} %get-tuple-element.15) | data formatting | bytes 2048
  115.8 2.3 %copy.17 = f32[1024,256]{1,0:T(8,128)} copy(f32[1024,256]{1,0:T(8,128)} %get-tuple-element.17) | data formatting | bytes 2097152

commit v2 on v1

--- a/solution.py
+++ b/solution.py
@@ -69,18 +69,21 @@
 
 
 def kernel(
-    tokens,
+    tokens_hbm,
     w_in,
     w_out,
     w_proj,
-    pos_embed,
+    pos_hbm,
     pos_ids,
     lengths,
-    neg_embed,
+    neg_hbm,
     neg_ids,
     loss_ref,
     dneg_ref,
     dproj_ref,
+    tokens,
+    pos_embed,
+    neg_embed,
     wkv,
     wq,
     wg,
@@ -99,7 +102,9 @@
     ids_all,
     cmask,
     kept,
+    wt,
     pos_t,
+    neg_unit,
     cs,
     cr,
     own,
@@ -107,14 +112,19 @@
     xr,
     ys,
     yr,
+    ybs,
+    ybr,
+    xbs,
+    xbr,
+    neg_t,
     zs,
     zr,
+    term,
     pcs,
     pcr,
-    pown,
-    pzs,
+    pxs,
+    pxr,
     pzr,
-    pxr,
     fin,
     w_sem,
     kv_sem,
@@ -125,10 +135,12 @@
     c_sem,
     x_sem,
     y_sem,
+    yb_sem,
+    xb_sem,
     z_sem,
     pc_sem,
+    px_sem,
     pz_sem,
-    px_sem,
     f_sem,
     fc_sem,
 ):
@@ -168,12 +180,18 @@
     load_g = pltpu.make_async_copy(w_in.at[:, pl.ds(0, WIDTH)], wg, w_sem.at[24])
     load_o = pltpu.make_async_copy(w_out, wo, w_sem.at[25])
     load_p = pltpu.make_async_copy(w_proj, wp, w_sem.at[26])
+    load_t = pltpu.make_async_copy(tokens_hbm, tokens, w_sem.at[27])
+    load_n = pltpu.make_async_copy(neg_hbm, neg_embed, w_sem.at[28])
+    load_pos = pltpu.make_async_copy(pos_hbm, pos_embed, w_sem.at[29])
+    load_t.start()
     for i in range(8):
         for c in load_kv(far_first(i)):
             c.start()
     for i in range(4):
         load_q(i, 0).start()
         load_q(i, 1).start()
+    load_n.start()
+    load_pos.start()
     load_g.start()
     load_o.start()
     load_p.start()
@@ -193,6 +211,8 @@
         pl.semaphore_signal(
             barrier, inc=1, device_id={"batch": 1 - b, "pool": 2 * k + core}, device_id_type=MESH
         )
+
+    load_t.wait()
 
     @pl.loop(0, 4)
     def _(i):
@@ -202,8 +222,6 @@
     length = lengths[0]
     row_pos = s * ROWS + lax.broadcasted_iota(jnp.int32, (ROWS, 1), 0)
     row_valid = row_pos < length
-
-    pl.semaphore_wait(barrier, (SEQ - 1) + (POOL - 1) + POOL // 2)
 
     def send_kv(k):
         return remote(
@@ -224,16 +242,16 @@
         keys = both[:, :HEAD].astype(BF16)
         values = jnp.where(row_valid, both[:, HEAD:], 0.0).astype(BF16)
 
-        @pl.when(i < SEQ - 1)
-        def _():
-            kvs[k, 0] = keys
-            kvs[k, 1] = values
-            send_kv(k).start()
-
-        @pl.when(i == SEQ - 1)
-        def _():
-            kvr[s, 0] = keys
-            kvr[s, 1] = values
+        kvs[k, 0] = keys
+        kvs[k, 1] = values
+
+    pl.semaphore_wait(barrier, (SEQ - 1) + (POOL - 1) + POOL // 2)
+
+    @pl.loop(0, SEQ - 1)
+    def _(i):
+        send_kv(far_first(i)).start()
+
+    kvr[s] = kvs[0]
 
     def send_q(k):
         return remote(qs.at[k], qr.at[s], q_sem.at[0, k], q_sem.at[1, k], seq=(s + k) % SEQ)
@@ -262,9 +280,11 @@
         def _():
             qr[s] = both[:, HEAD:]
 
+    load_n.wait()
     neg = neg_embed[...].astype(F32)
     neg_norm = jnp.sqrt(jnp.sum(neg * neg, axis=-1, keepdims=True) + UNIT_EPSILON)
-    negs[p] = (neg / neg_norm).astype(BF16)
+    neg_unit[...] = neg / neg_norm
+    negs[p] = neg_unit[...].astype(BF16)
     ids_all[p] = neg_ids[...]
 
     def send_ids(k):
@@ -296,6 +316,7 @@
         cols = pl.ds(pl.multiple_of(i * 256, 256), 256)
         gate[:, cols] = silu(dot(normed[...], wg[:, cols])).astype(BF16)
 
+    load_pos.wait()
     pos = jnp.transpose(pos_embed[...].astype(F32))
     pos_t[...] = pos / jnp.sqrt(jnp.sum(pos * pos, axis=0, keepdims=True) + UNIT_EPSILON)
     pos_row = pos_ids[...]
@@ -370,7 +391,7 @@
             recv_negs(k).wait_recv()
 
         src = (p + POOL - k) % POOL
-        negs_t[src] = jnp.transpose(negs[src])
+        negs_t[:, pl.ds(pl.multiple_of(src * ROWS, ROWS), ROWS)] = jnp.transpose(negs[src])
 
     load_o.wait()
     load_p.wait()
@@ -404,188 +425,218 @@
     share = jnp.where(valid, 1.0 / (total * HIST), 0.0)
     pos_weight = jnp.where(valid, pos_exp / total - 1.0, 0.0) * (1.0 / HIST)
 
-    def send_c(m):
-        return remote(cs.at[m], cr.at[m], c_sem.at[0, m], c_sem.at[1, m], pool=sibling)
-
-    def other_core(m, rows_t):
-        j = 2 * m + 1 - core
-        weight = (kept[j] * share).astype(BF16)
-        cs[m] = (dot(weight, out_hat) * (1.0 / WARMTH)).astype(BF16)
-        send_c(m).start()
-        return rows_t + dot(negs_t[j], weight)
-
-    def this_core(m, rows_t):
-        j = 2 * m + core
-        weight = (kept[j] * share).astype(BF16)
-        own[m] = dot(weight, out_hat) * (1.0 / WARMTH)
-        return rows_t + dot(negs_t[j], weight)
-
-    rows_t = lax.fori_loop(0, 8, other_core, jnp.zeros((EMBED, ROWS), F32))
-    rows_t = lax.fori_loop(0, 8, this_core, rows_t)
-
+    @pl.loop(0, POOL)
+    def _(j):
+        wt[pl.ds(pl.multiple_of(j * ROWS, ROWS), ROWS), :] = (kept[j] * share).astype(BF16)
+
+    rows_t = dot(negs_t[...], wt[...])
     grad_t = (pos_weight * pos_t[...] + rows_t) * (1.0 / WARMTH)
     d_out = jnp.transpose(
         (grad_t - unit_t * jnp.sum(unit_t * grad_t, axis=0, keepdims=True)) / norm_t
     ).astype(BF16)
-    term = dot_tn(layer_out, d_out)
-    half_rows = WIDTH // 2
-
-    for c in range(2):
-        part = term[c * half_rows : (c + 1) * half_rows]
-
-        @pl.when(core == c)
-        def _():
-            pown[...] = part
-
-        @pl.when(core != c)
-        def _():
-            pcs[...] = part.astype(BF16)
-
+    term[...] = dot_tn(layer_out, d_out)
+
+    half = WIDTH // 2
+    mine = pl.ds(pl.multiple_of(core * half, half), half)
+    theirs = pl.ds(pl.multiple_of((1 - core) * half, half), half)
+    pcs[...] = term[theirs, :].astype(BF16)
     send_pc = remote(pcs, pcr, pc_sem.at[0], pc_sem.at[1], pool=sibling)
     send_pc.start()
 
+    def place(n):
+        y_at = (y + 1 + n // 2) % 4
+        x_at = xlo + (1 - n % 2) * (1 - 2 * xlo)
+        return y_at, x_at
+
+    def send_c(m):
+        return remote(cs.at[m], cr.at[m], c_sem.at[0, m], c_sem.at[1, m], pool=sibling)
+
+    def portion(j):
+        weight = wt[pl.ds(pl.multiple_of(j * ROWS, ROWS), ROWS), :]
+        return dot(weight, out_hat) * (1.0 / WARMTH)
+
+    @pl.loop(0, 8)
+    def _(n):
+        y_at, x_at = place(n)
+        m = 2 * y_at + x_at
+        cs[m] = portion(2 * m + 1 - core).astype(BF16)
+        send_c(m).start()
+
+    def plane(q):
+        return {"batch": q // 8, "pool": 2 * (q % 8) + core}
+
+    def send_px(k):
+        q = (q_own + k) % GRID
+        return remote(
+            pxs.at[pl.ds(pl.multiple_of(q * 32, 32), 32), :],
+            pxr.at[q_own],
+            px_sem.at[0, k],
+            px_sem.at[1, k],
+            **plane(q),
+        )
+
+    def recv_px(k):
+        q = (q_own + GRID - k) % GRID
+        return remote(
+            pxs.at[pl.ds(0, 32), :], pxr.at[q], px_sem.at[0, k], px_sem.at[1, k], **plane(q)
+        )
+
+    send_pc.wait_recv()
+    pxs[...] = (term[mine, :] + pcr[...].astype(F32)).astype(BF16)
+
+    @pl.loop(1, GRID)
+    def _(k):
+        send_px(k).start()
+
+    pxr[q_own] = pxs[pl.ds(pl.multiple_of(q_own * 32, 32), 32), :]
+
     def send_x(i):
         return remote(xs.at[i], xr.at[i], x_sem.at[0, i], x_sem.at[1, i], pool=across)
 
-    @pl.loop(0, 4)
-    def _(i):
-        m = 2 * i + 1 - xlo
+    def send_yb(k):
+        return remote(
+            ybs.at[k], ybr.at[k], yb_sem.at[0, k], yb_sem.at[1, k], pool=((y + k) % 4) * 4 + p % 4
+        )
+
+    @pl.loop(0, 8)
+    def _(n):
+        y_at, x_at = place(n)
+        m = 2 * y_at + x_at
+        mixed = portion(2 * m + core)
         send_c(m).wait_recv()
-        xs[i] = (own[m] + cr[m].astype(F32)).astype(BF16)
-        send_x(i).start()
+        mixed = mixed + cr[m].astype(F32)
+        own[m] = mixed
+
+        @pl.when(n % 2 == 0)
+        def _():
+            xs[y_at] = mixed[:128].astype(BF16)
+            send_x(y_at).start()
+
+        @pl.when(n < 6)
+        def _():
+            ybs[1 + n // 2, x_at] = mixed[128:].astype(BF16)
+
+        @pl.when((n < 6) & (n % 2 == 1))
+        def _():
+            send_yb(1 + n // 2).start()
 
     def send_pz(k):
-        return remote(
-            pzs.at[k], pzr.at[k], pz_sem.at[0, k], pz_sem.at[1, k], seq=(s + k) % SEQ
-        )
-
-    send_pc.wait_recv()
+        return remote(pzr.at[s], pzr.at[s], pz_sem.at[0, k], pz_sem.at[1, k], seq=(s + k) % SEQ)
+
+    def recv_pz(k):
+        src = (s + SEQ - k) % SEQ
+        return remote(pzr.at[src], pzr.at[src], pz_sem.at[0, k], pz_sem.at[1, k], seq=src)
+
+    @pl.loop(1, GRID)
+    def _(k):
+        recv_px(k).wait_recv()
+
+    block = pxr[0].astype(F32)
+    for q in range(1, GRID):
+        block = block + pxr[q].astype(F32)
+    pzr[s] = block.astype(BF16)
 
     @pl.loop(1, SEQ)
     def _(k):
-        rows = pl.ds(pl.multiple_of(((s + k) % SEQ) * 64, 64), 64)
-        pzs[k] = (pown[rows, :] + pcr[rows, :].astype(F32)).astype(BF16)
         send_pz(k).start()
-
-    own_rows = pl.ds(pl.multiple_of(s * 64, 64), 64)
-    block = pown[own_rows, :] + pcr[own_rows, :].astype(F32)
 
     def send_y(k):
         return remote(
             ys.at[k], yr.at[k], y_sem.at[0, k], y_sem.at[1, k], pool=((y + k) % 4) * 4 + p % 4
         )
 
-    @pl.loop(0, 4)
-    def _(i):
-        m = 2 * i + xlo
-        send_c(m).wait_recv()
-        own[m] = own[m] + cr[m].astype(F32)
+    send_xb = remote(xbs, xbr, xb_sem.at[0], xb_sem.at[1], pool=across)
 
     @pl.loop(1, 4)
     def _(k):
         i = (y + k) % 4
-        m = 2 * i + xlo
         send_x(i).wait_recv()
-        ys[k] = (own[m] + xr[i].astype(F32)).astype(BF16)
+        ys[k] = (own[2 * i + xlo, :128] + xr[i].astype(F32)).astype(BF16)
         send_y(k).start()
 
+    lower_theirs = own[2 * y + 1 - xlo, 128:]
+    lower = own[2 * y + xlo, 128:]
+    for k in range(1, 4):
+        send_yb(k).wait_recv()
+        lower_theirs = lower_theirs + ybr[k, 1 - xlo].astype(F32)
+        lower = lower + ybr[k, xlo].astype(F32)
+    xbs[...] = lower_theirs.astype(BF16)
+    send_xb.start()
     send_x(y).wait_recv()
-    neg_sum = own[2 * y + xlo] + xr[y].astype(F32)
-
-    def send_px(k):
-        q = (q_own + k) % GRID
-        return remote(
-            pxr.at[q_own],
-            pxr.at[q_own],
-            px_sem.at[0, k],
-            px_sem.at[1, k],
-            batch=q // 8,
-            pool=2 * (q % 8) + core,
-        )
-
-    def recv_px(k):
+    own[2 * y + xlo, :128] = own[2 * y + xlo, :128] + xr[y].astype(F32)
+    own[2 * y + xlo, 128:] = lower
+
+    @pl.loop(1, SEQ)
+    def _(k):
+        recv_pz(k).wait_recv()
+
+    whole = pzr[0].astype(F32)
+    for z in range(1, SEQ):
+        whole = whole + pzr[z].astype(F32)
+    fin[core * GRID + q_own] = whole.astype(BF16)
+
+    def send_f(k):
+        at = core * GRID + q_own
+        return remote(fin.at[at], fin.at[at], f_sem.at[0, k], f_sem.at[1, k], **plane((q_own + k) % GRID))
+
+    def recv_f(k):
         q = (q_own + GRID - k) % GRID
-        return remote(
-            pxr.at[q], pxr.at[q], px_sem.at[0, k], px_sem.at[1, k], batch=q // 8, pool=2 * (q % 8) + core
-        )
-
-    for k in range(1, SEQ):
-        send_pz(k).wait_recv()
-        block = block + pzr[k].astype(F32)
-    pxr[q_own] = block.astype(BF16)
+        at = core * GRID + q
+        return remote(fin.at[at], fin.at[at], f_sem.at[0, k], f_sem.at[1, k], **plane(q))
+
+    def send_fc(k):
+        at = core * GRID + (q_own + GRID - k) % GRID
+        return remote(fin.at[at], fin.at[at], fc_sem.at[0, k], fc_sem.at[1, k], pool=sibling)
+
+    def recv_fc(k):
+        at = (1 - core) * GRID + (q_own + GRID - k) % GRID
+        return remote(fin.at[at], fin.at[at], fc_sem.at[0, k], fc_sem.at[1, k], pool=sibling)
 
     @pl.loop(1, GRID)
     def _(k):
-        send_px(k).start()
+        send_f(k).start()
+
+    send_fc(0).start()
 
     def send_z(k):
         return remote(zs.at[k], zr.at[k], z_sem.at[0, k], z_sem.at[1, k], seq=(s + k) % SEQ)
 
+    upper = own[2 * y + xlo, :128]
     for k in range(1, 4):
         send_y(k).wait_recv()
-        neg_sum = neg_sum + yr[k].astype(F32)
+        upper = upper + yr[k].astype(F32)
+    send_xb.wait_recv()
+    lower = own[2 * y + xlo, 128:] + xbr[...].astype(F32)
+    neg_sum = jnp.concatenate([upper, lower], axis=0)
     neg = neg_embed[...].astype(F32)
     neg_norm = jnp.sqrt(jnp.sum(neg * neg, axis=-1, keepdims=True) + UNIT_EPSILON)
-    neg_unit = neg / neg_norm
-    neg_term = (neg_sum - neg_unit * jnp.sum(neg_unit * neg_sum, axis=-1, keepdims=True)) / neg_norm
-    cr_t = jnp.transpose(neg_term)
-    own[0] = cr_t
+    unit = neg_unit[...]
+    neg_t[...] = jnp.transpose(
+        (neg_sum - unit * jnp.sum(unit * neg_sum, axis=-1, keepdims=True)) / neg_norm
+    )
 
     @pl.loop(1, SEQ)
     def _(k):
         rows = pl.ds(pl.multiple_of(((s + k) % SEQ) * 32, 32), 32)
-        zs[k] = own[0, rows, :].astype(BF16)
+        zs[k] = neg_t[rows, :].astype(BF16)
         send_z(k).start()
 
     @pl.loop(1, GRID)
     def _(k):
-        recv_px(k).wait_recv()
-
-    whole = pxr[0].astype(F32)
-    for q in range(1, GRID):
-        whole = whole + pxr[q].astype(F32)
-    fin[core * SEQ + s] = whole.astype(BF16)
-
-    def send_f(k):
-        at = core * SEQ + s
-        return remote(fin.at[at], fin.at[at], f_sem.at[0, k], f_sem.at[1, k], seq=(s + k) % SEQ)
-
-    def recv_f(k):
-        at = core * SEQ + (s + SEQ - k) % SEQ
-        return remote(fin.at[at], fin.at[at], f_sem.at[0, k], f_sem.at[1, k], seq=(s + k) % SEQ)
-
-    def send_fc(k):
-        at = core * SEQ + (s + SEQ - k) % SEQ
-        return remote(fin.at[at], fin.at[at], fc_sem.at[0, k], fc_sem.at[1, k], pool=sibling)
-
-    def recv_fc(k):
-        at = (1 - core) * SEQ + (s + SEQ - k) % SEQ
-        return remote(fin.at[at], fin.at[at], fc_sem.at[0, k], fc_sem.at[1, k], pool=sibling)
-
-    @pl.loop(1, SEQ)
-    def _(k):
-        send_f(k).start()
-
-    send_fc(0).start()
-
-    part = own[0, pl.ds(pl.multiple_of(s * 32, 32), 32), :]
+        recv_f(k).wait_recv()
+        send_fc(k).start()
+
+    part = neg_t[pl.ds(pl.multiple_of(s * 32, 32), 32), :]
     for k in range(1, SEQ):
         send_z(k).wait_recv()
         part = part + zr[k].astype(F32)
-    dneg_ref[...] = jnp.transpose(part)
-
-    @pl.loop(1, SEQ)
-    def _(k):
-        recv_f(k).wait_recv()
-        send_fc(k).start()
-
-    @pl.loop(0, SEQ)
+    dneg_ref[...] = part
+
+    @pl.loop(0, GRID)
     def _(k):
         recv_fc(k).wait_recv()
 
-    @pl.loop(0, 16)
-    def _(i):
-        dproj_ref[pl.ds(pl.multiple_of(i * 64, 64), 64), :] = fin[i].astype(F32)
+    dproj_ref[...] = fin[...]
 
     @pl.loop(1, SEQ)
     def _(k):
@@ -594,18 +645,21 @@
         send_o(k).wait_send()
         send_pz(k).wait_send()
         send_z(k).wait_send()
-        send_f(k).wait_send()
 
     @pl.loop(1, POOL)
     def _(k):
         send_ids(k).wait_send()
         send_negs(k).wait_send()
         send_px(k).wait_send()
+        send_f(k).wait_send()
+
+    @pl.loop(0, GRID)
+    def _(k):
+        send_fc(k).wait_send()
 
     @pl.loop(0, 8)
     def _(m):
         send_c(m).wait_send()
-        send_fc(m).wait_send()
 
     @pl.loop(0, 4)
     def _(i):
@@ -614,8 +668,16 @@
     @pl.loop(1, 4)
     def _(k):
         send_y(k).wait_send()
-
+        send_yb(k).wait_send()
+
+    send_xb.wait_send()
     send_pc.wait_send()
+
+
+def finish(loss, dneg_t, dproj, loss_out, dneg_out, dproj_out):
+    loss_out[...] = loss[...]
+    dneg_out[...] = dneg_t[...]
+    dproj_out[...] = dproj[...].astype(F32)
 
 
 def body(tokens, w_in, w_out, w_proj, pos_embed, pos_ids, lengths, neg_embed, neg_ids):
@@ -623,16 +685,19 @@
     hbm = pl.BlockSpec(memory_space=pl.ANY)
     smem = pl.BlockSpec(memory_space=pltpu.SMEM)
     dma = pltpu.SemaphoreType.DMA
-    loss, d_neg, d_proj = pl.pallas_call(
+    loss, dneg_t, dproj = pl.pallas_call(
         kernel,
         out_shape=(
             jax.ShapeDtypeStruct((1, ROWS), F32),
-            jax.ShapeDtypeStruct((ROWS, EMBED // SEQ), F32),
-            jax.ShapeDtypeStruct((WIDTH, EMBED), F32),
+            jax.ShapeDtypeStruct((EMBED // SEQ, ROWS), F32),
+            jax.ShapeDtypeStruct((2 * GRID, 32, EMBED), BF16),
         ),
-        in_specs=[vmem, hbm, hbm, hbm, vmem, vmem, smem, vmem, vmem],
+        in_specs=[hbm, hbm, hbm, hbm, hbm, vmem, smem, hbm, vmem],
         out_specs=(vmem, vmem, vmem),
         scratch_shapes=[
+            pltpu.VMEM((ROWS, WIDTH), BF16),
+            pltpu.VMEM((ROWS, EMBED), BF16),
+            pltpu.VMEM((ROWS, EMBED), BF16),
             pltpu.VMEM((8, WIDTH, 256), BF16),
             pltpu.VMEM((4, WIDTH, 256), BF16),
             pltpu.VMEM((WIDTH, WIDTH), BF16),
@@ -647,28 +712,35 @@
             pltpu.VMEM((SEQ, ROWS, HEAD), BF16),
             pltpu.VMEM((ROWS, WIDTH), BF16),
             pltpu.VMEM((POOL, ROWS, EMBED), BF16),
-            pltpu.VMEM((POOL, EMBED, ROWS), BF16),
+            pltpu.VMEM((EMBED, POOL * ROWS), BF16),
             pltpu.VMEM((POOL, 1, ROWS), jnp.int32),
             pltpu.VMEM((POOL, ROWS, ROWS), F32),
             pltpu.VMEM((POOL, ROWS, ROWS), F32),
+            pltpu.VMEM((POOL * ROWS, ROWS), BF16),
             pltpu.VMEM((EMBED, ROWS), F32),
+            pltpu.VMEM((ROWS, EMBED), F32),
             pltpu.VMEM((8, ROWS, EMBED), BF16),
             pltpu.VMEM((8, ROWS, EMBED), BF16),
             pltpu.VMEM((8, ROWS, EMBED), F32),
-            pltpu.VMEM((4, ROWS, EMBED), BF16),
-            pltpu.VMEM((4, ROWS, EMBED), BF16),
-            pltpu.VMEM((4, ROWS, EMBED), BF16),
-            pltpu.VMEM((4, ROWS, EMBED), BF16),
+            pltpu.VMEM((4, 128, EMBED), BF16),
+            pltpu.VMEM((4, 128, EMBED), BF16),
+            pltpu.VMEM((4, 128, EMBED), BF16),
+            pltpu.VMEM((4, 128, EMBED), BF16),
+            pltpu.VMEM((4, 2, 128, EMBED), BF16),
+            pltpu.VMEM((4, 2, 128, EMBED), BF16),
+            pltpu.VMEM((128, EMBED), BF16),
+            pltpu.VMEM((128, EMBED), BF16),
+            pltpu.VMEM((EMBED, ROWS), F32),
             pltpu.VMEM((SEQ, 32, ROWS), BF16),
             pltpu.VMEM((SEQ, 32, ROWS), BF16),
+            pltpu.VMEM((WIDTH, EMBED), F32),
             pltpu.VMEM((WIDTH // 2, EMBED), BF16),
             pltpu.VMEM((WIDTH // 2, EMBED), BF16),
-            pltpu.VMEM((WIDTH // 2, EMBED), F32),
-            pltpu.VMEM((SEQ, 64, EMBED), BF16),
-            pltpu.VMEM((SEQ, 64, EMBED), BF16),
-            pltpu.VMEM((GRID, 64, EMBED), BF16),
-            pltpu.VMEM((16, 64, EMBED), BF16),
-            dma((27,)),
+            pltpu.VMEM((WIDTH // 2, EMBED), BF16),
+            pltpu.VMEM((GRID, 32, EMBED), BF16),
+            pltpu.VMEM((SEQ, 32, EMBED), BF16),
+            pltpu.VMEM((2 * GRID, 32, EMBED), BF16),
+            dma((30,)),
             dma((2, SEQ)),
             dma((2, SEQ)),
             dma((2, SEQ)),
@@ -677,12 +749,14 @@
             dma((2, 8)),
             dma((2, 4)),
             dma((2, 4)),
+            dma((2, 4)),
+            dma((2,)),
             dma((2, SEQ)),
             dma((2,)),
+            dma((2, GRID)),
             dma((2, SEQ)),
             dma((2, GRID)),
-            dma((2, SEQ)),
-            dma((2, SEQ)),
+            dma((2, GRID)),
         ],
         compiler_params=pltpu.CompilerParams(
             collective_id=0, has_side_effects=True, vmem_limit_bytes=56 * 1024 * 1024
@@ -698,7 +772,17 @@
         neg_embed[0],
         neg_ids,
     )
-    return (loss, d_neg[None], d_proj)
+    loss, dneg_t, dproj = pl.pallas_call(
+        finish,
+        out_shape=(
+            jax.ShapeDtypeStruct((1, ROWS), F32),
+            jax.ShapeDtypeStruct((EMBED // SEQ, ROWS), F32),
+            jax.ShapeDtypeStruct((WIDTH, EMBED), F32),
+        ),
+        in_specs=[vmem, vmem, vmem],
+        out_specs=(vmem, vmem, vmem),
+    )(loss, dneg_t, dproj.reshape(WIDTH, EMBED))
+    return (loss, jnp.transpose(dneg_t)[None], dproj)
 
 
 def solution(mesh):

time: 118 us -> 95.9 us (0.81)
  Pallas kernels: 112 us -> 94.5 us
  local copies, waits for them, and re-layouts: 5.07 us -> 0 us
    pallas_call x1, Pallas kernels: 112 us -> 92.4 us  [body(): pl.pallas_call(kernel, out_shape=(jax.ShapeDtypeStruct((1, ROWS), F32), j...]
    unnamed x3 -> x0, local copies, waits for them, and re-layouts: 5.07 us -> none
    pallas_call x0 -> x1, Pallas kernels: none -> 2.11 us  [body(): pl.pallas_call(finish, out_shape=(jax.ShapeDtypeStruct((1, ROWS), F32), j...]
where the time goes in v2:
time: 95.9 us; the launch traced here: 95.8 us
  Pallas kernels  94.5 us (99%)
  between operations  1.29 us (1%)
    pallas_call x1, Pallas kernels, body(): pl.pallas_call(kernel, out_shape=(jax.ShapeDtypeStruct((1, ROWS), F32), j...  92.4 us
    pallas_call x1, Pallas kernels, body(): pl.pallas_call(finish, out_shape=(jax.ShapeDtypeStruct((1, ROWS), F32), j...  2.11 us

profile of v2, /device:TPU:1, one launch (start us, length us, event | category | flops | bytes accessed | tf_op | source)
XLA Modules:
  0.0 95.8 jit_solution(6301265713863702204)
XLA Ops:
  1.3 92.4 %shard_map.112 = (f32[1,256]{1,0:T(1,128)}, f32[32,256]{1,0:T(8,128)}, bf16[32,32,256]{2,1,0:T(8,128)(2,1)}) custom-call(bf16[256,1024]{1,0:T(8,128)(2,1)} %bitcast.7, bf16[1024,4096]{1,0:T(8,128)(2,1)} %w_in.1, bf16[1024,1024]{1,0:T(8,128)(2,1)} %w_out.1, bf16[1024,256]{1,0:T(8,128)(2,1)} %w_proj.1, bf16[256,256]{1,0:T(8,128)(2,1)} %bitcast.9, ...), custom_call_target="tpu_custom_call" | custom-call | tf_op jit(solution)/shard_map/pallas_call | solution.py:688
  93.7 2.1 %shard_map.113 = (f32[1,256]{1,0:T(1,128)}, f32[32,256]{1,0:T(8,128)}, f32[1024,256]{1,0:T(8,128)}) custom-call(f32[1,256]{1,0:T(1,128)} %get-tuple-element.9.loss, f32[32,256]{1,0:T(8,128)} %get-tuple-element.10.dneg_t, bf16[1024,256]{1,0:T(8,128)(2,1)} %bitcast.8), custom_call_target="tpu_custom_call" | custom-call | tf_op jit(solution)/shard_map/pallas_call | solution.py:775

commit v3 on v2

--- a/solution.py
+++ b/solution.py
@@ -10,6 +10,7 @@
 HEADS = 8
 HEAD = 128
 ROWS = 256
+HALF = 128
 WIDTH = 1024
 EMBED = 256
 SEQ = 8
@@ -58,6 +59,12 @@
     return math.log(ITEMS + 1.0) / (2.0 * z * series)
 
 
+STEPS = sorted(
+    [(dx, dy) for dx in range(4) for dy in range(4) if dx or dy],
+    key=lambda d: -(min(d[0], 4 - d[0]) + min(d[1], 4 - d[1])),
+)
+
+
 def far_first(i):
     return 4 + (1 - 2 * (i % 2)) * ((i + 1) // 2)
 
@@ -74,16 +81,19 @@
     w_out,
     w_proj,
     pos_hbm,
-    pos_ids,
-    lengths,
+    pos_ids_hbm,
+    lengths_hbm,
     neg_hbm,
-    neg_ids,
+    neg_ids_hbm,
     loss_ref,
     dneg_ref,
     dproj_ref,
     tokens,
     pos_embed,
     neg_embed,
+    pos_ids,
+    neg_ids,
+    lengths,
     wkv,
     wq,
     wg,
@@ -103,6 +113,9 @@
     cmask,
     kept,
     wt,
+    layer_out,
+    out_hat,
+    d_out,
     pos_t,
     neg_unit,
     cs,
@@ -126,6 +139,8 @@
     pxr,
     pzr,
     fin,
+    loss,
+    dneg,
     w_sem,
     kv_sem,
     q_sem,
@@ -143,6 +158,7 @@
     pz_sem,
     f_sem,
     fc_sem,
+    out_sem,
 ):
     b = lax.axis_index("batch")
     s = lax.axis_index("seq")
@@ -154,6 +170,11 @@
     across = p + 2 - 4 * xlo
     q_own = b * 8 + p // 2
 
+    load_ids = [
+        pltpu.make_async_copy(pos_ids_hbm, pos_ids, w_sem.at[30]),
+        pltpu.make_async_copy(neg_ids_hbm, neg_ids, w_sem.at[31]),
+        pltpu.make_async_copy(lengths_hbm, lengths, w_sem.at[32]),
+    ]
     def load_kv(k):
         h = (s + k) % SEQ
         return [
@@ -183,75 +204,78 @@
     load_t = pltpu.make_async_copy(tokens_hbm, tokens, w_sem.at[27])
     load_n = pltpu.make_async_copy(neg_hbm, neg_embed, w_sem.at[28])
     load_pos = pltpu.make_async_copy(pos_hbm, pos_embed, w_sem.at[29])
+    barrier = pltpu.get_barrier_semaphore()
+
+    @pl.loop(1, SEQ)
+    def _(k):
+        pl.semaphore_signal(barrier, inc=1, device_id={"seq": (s + k) % SEQ}, device_id_type=MESH)
+
+    @pl.loop(1, POOL)
+    def _(k):
+        pl.semaphore_signal(barrier, inc=1, device_id={"pool": (p + k) % POOL}, device_id_type=MESH)
+
+    @pl.loop(0, POOL // 2)
+    def _(k):
+        pl.semaphore_signal(
+            barrier, inc=1, device_id={"batch": 1 - b, "pool": 2 * k + core}, device_id_type=MESH
+        )
+
     load_t.start()
-    for i in range(8):
+    for c in load_kv(4) + load_ids:
+        c.start()
+    for i in range(1, 8):
         for c in load_kv(far_first(i)):
             c.start()
     for i in range(4):
         load_q(i, 0).start()
         load_q(i, 1).start()
+
+    load_t.wait()
+
+    normed[...] = layer_norm(tokens[...].astype(F32)).astype(BF16)
+
+    for c in load_ids:
+        c.wait()
+    length = lengths[0]
+    row_pos = s * ROWS + lax.broadcasted_iota(jnp.int32, (ROWS, 1), 0)
+    row_valid = row_pos < length
+
+    def send_kv(k):
+        return remote(
+            kvs.at[k], kvr.at[s], kv_sem.at[0, k], kv_sem.at[1, k], seq=(s + k) % SEQ
+        )
+
+    def recv_kv(k):
+        return remote(
+            kvs.at[k], kvr.at[(s + SEQ - k) % SEQ], kv_sem.at[0, k], kv_sem.at[1, k], seq=(s + k) % SEQ
+        )
+
+    def make_kv(k):
+        for c in load_kv(k):
+            c.wait()
+        both = silu(dot(normed[...], wkv[k]))
+        kvs[k, 0] = both[:, :HEAD].astype(BF16)
+        kvs[k, 1] = jnp.where(row_valid, both[:, HEAD:], 0.0).astype(BF16)
+
+    make_kv(4)
+    pl.semaphore_wait(barrier, (SEQ - 1) + (POOL - 1) + POOL // 2)
+    send_kv(4).start()
+
+    @pl.loop(1, SEQ)
+    def _(i):
+        k = far_first(i)
+        make_kv(k)
+
+        @pl.when(i < SEQ - 1)
+        def _():
+            send_kv(k).start()
+
+    kvr[s] = kvs[0]
     load_n.start()
     load_pos.start()
     load_g.start()
     load_o.start()
     load_p.start()
-
-    barrier = pltpu.get_barrier_semaphore()
-
-    @pl.loop(1, SEQ)
-    def _(k):
-        pl.semaphore_signal(barrier, inc=1, device_id={"seq": (s + k) % SEQ}, device_id_type=MESH)
-
-    @pl.loop(1, POOL)
-    def _(k):
-        pl.semaphore_signal(barrier, inc=1, device_id={"pool": (p + k) % POOL}, device_id_type=MESH)
-
-    @pl.loop(0, POOL // 2)
-    def _(k):
-        pl.semaphore_signal(
-            barrier, inc=1, device_id={"batch": 1 - b, "pool": 2 * k + core}, device_id_type=MESH
-        )
-
-    load_t.wait()
-
-    @pl.loop(0, 4)
-    def _(i):
-        rows = pl.ds(pl.multiple_of(i * 64, 64), 64)
-        normed[rows, :] = layer_norm(tokens[rows, :].astype(F32)).astype(BF16)
-
-    length = lengths[0]
-    row_pos = s * ROWS + lax.broadcasted_iota(jnp.int32, (ROWS, 1), 0)
-    row_valid = row_pos < length
-
-    def send_kv(k):
-        return remote(
-            kvs.at[k], kvr.at[s], kv_sem.at[0, k], kv_sem.at[1, k], seq=(s + k) % SEQ
-        )
-
-    def recv_kv(k):
-        return remote(
-            kvs.at[k], kvr.at[(s + SEQ - k) % SEQ], kv_sem.at[0, k], kv_sem.at[1, k], seq=(s + k) % SEQ
-        )
-
-    @pl.loop(0, SEQ)
-    def _(i):
-        k = far_first(i)
-        for c in load_kv(k):
-            c.wait()
-        both = silu(dot(normed[...], wkv[k]))
-        keys = both[:, :HEAD].astype(BF16)
-        values = jnp.where(row_valid, both[:, HEAD:], 0.0).astype(BF16)
-
-        kvs[k, 0] = keys
-        kvs[k, 1] = values
-
-    pl.semaphore_wait(barrier, (SEQ - 1) + (POOL - 1) + POOL // 2)
-
-    @pl.loop(0, SEQ - 1)
-    def _(i):
-        send_kv(far_first(i)).start()
-
-    kvr[s] = kvs[0]
 
     def send_q(k):
         return remote(qs.at[k], qr.at[s], q_sem.at[0, k], q_sem.at[1, k], seq=(s + k) % SEQ)
@@ -331,13 +355,27 @@
     for j in range(POOL):
         cmask[j] = jnp.where(ids_col[:, j : j + 1] != pos_row, factor[:, j : j + 1], 0.0)
 
-    def send_o(k):
-        dst = (s + SEQ - k) % SEQ
-        return remote(osend.at[k], orecv.at[s], o_sem.at[0, k], o_sem.at[1, k], seq=dst)
-
-    def recv_o(k):
+    def half_rows(h):
+        return pl.ds(h * HALF, HALF)
+
+    def send_o(k, h):
+        return remote(
+            osend.at[k, half_rows(h)],
+            orecv.at[s, half_rows(h)],
+            o_sem.at[h, 0, k],
+            o_sem.at[h, 1, k],
+            seq=(s + SEQ - k) % SEQ,
+        )
+
+    def recv_o(k, h):
         src = (s + k) % SEQ
-        return remote(osend.at[k], orecv.at[src], o_sem.at[0, k], o_sem.at[1, k], seq=src)
+        return remote(
+            osend.at[k, half_rows(h)],
+            orecv.at[src, half_rows(h)],
+            o_sem.at[h, 0, k],
+            o_sem.at[h, 1, k],
+            seq=src,
+        )
 
     @pl.loop(1, SEQ)
     def _(k):
@@ -361,29 +399,31 @@
             return half + half * jnp.tanh(half)
 
         def group(g, total):
-            return (
-                total
-                + dot(weights(2 * g).astype(BF16), kvr[2 * g, 1])
-                + dot(weights(2 * g + 1).astype(BF16), kvr[2 * g + 1, 1])
-            )
-
-        total = lax.fori_loop(0, a // 2, group, jnp.zeros((ROWS, HEAD), F32))
-        last = 2 * (a // 2)
+            for u in range(4):
+                total = total + dot(weights(4 * g + u).astype(BF16), kvr[4 * g + u, 1])
+            return total
+
+        total = lax.fori_loop(0, a // 4, group, jnp.zeros((ROWS, HEAD), F32))
         t_pos = a * ROWS + lax.broadcasted_iota(jnp.int32, (ROWS, ROWS), 0)
         u_pos = lax.broadcasted_iota(jnp.int32, (ROWS, ROWS), 1)
-        for u in (last, last + 1):
+        for last in range(4):
+            u = 4 * (a // 4) + last
             seen = jnp.where(u * ROWS + u_pos <= t_pos, weights(u), 0.0).astype(BF16)
             total = total + dot(seen, kvr[u, 1])
 
         @pl.when(i > 0)
         def _():
             osend[k] = total.astype(BF16)
-            send_o(k).start()
+            send_o(k, 0).start()
 
         @pl.when(i == 0)
         def _():
             orecv[s] = total.astype(BF16)
 
+    @pl.loop(1, SEQ)
+    def _(i):
+        send_o(far_first(i - 1), 1).start()
+
     @pl.loop(0, POOL)
     def _(k):
         @pl.when(k > 0)
@@ -396,52 +436,63 @@
     load_o.wait()
     load_p.wait()
 
-    @pl.loop(1, SEQ)
-    def _(k):
-        recv_o(k).wait_recv()
-
-    attn = jnp.concatenate([orecv[h] for h in range(HEADS)], axis=1).astype(F32)
-    gated = (layer_norm(attn) * gate[...].astype(F32)).astype(BF16)
-    layer_out = (dot(gated, wo[...]) + tokens[...].astype(F32)).astype(BF16)
-    out = dot(layer_out, wp[...])
-    out_hat = (out * lax.rsqrt(jnp.sum(out * out, axis=-1, keepdims=True) + UNIT_EPSILON)).astype(BF16)
-    out_t = jnp.transpose(out)
-    norm_t = jnp.sqrt(jnp.sum(out_t * out_t, axis=0, keepdims=True) + UNIT_EPSILON)
-    unit_t = out_t / norm_t
-    hat_t = unit_t.astype(BF16)
-    pos_dot = jnp.sum(hat_t.astype(F32) * pos_t[...], axis=0, keepdims=True) * (1.0 / WARMTH)
-    pos_chance = inverse_chance(pos_row.astype(F32))
-    pos_logit = pos_dot + jnp.log(pos_chance)
-    pos_exp = jnp.exp(pos_logit)
-
-    def scores(j, total):
-        value = jnp.exp(dot(negs[j], hat_t) * (1.0 / WARMTH)) * cmask[j]
-        kept[j] = value
-        return total + jnp.sum(value, axis=0, keepdims=True)
-
-    total = lax.fori_loop(0, POOL, scores, jnp.zeros((1, ROWS), F32)) + pos_exp
-    valid = s * ROWS + lax.broadcasted_iota(jnp.int32, (1, ROWS), 1) < length
-    loss_ref[...] = jnp.where(valid, jnp.log(total) - pos_logit, 0.0)
-    share = jnp.where(valid, 1.0 / (total * HIST), 0.0)
-    pos_weight = jnp.where(valid, pos_exp / total - 1.0, 0.0) * (1.0 / HIST)
-
-    @pl.loop(0, POOL)
-    def _(j):
-        wt[pl.ds(pl.multiple_of(j * ROWS, ROWS), ROWS), :] = (kept[j] * share).astype(BF16)
-
-    rows_t = dot(negs_t[...], wt[...])
-    grad_t = (pos_weight * pos_t[...] + rows_t) * (1.0 / WARMTH)
-    d_out = jnp.transpose(
-        (grad_t - unit_t * jnp.sum(unit_t * grad_t, axis=0, keepdims=True)) / norm_t
-    ).astype(BF16)
-    term[...] = dot_tn(layer_out, d_out)
+    @pl.loop(0, 2)
+    def _(h):
+        start = pl.multiple_of(h * HALF, HALF)
+        rows = pl.ds(start, HALF)
+
+        @pl.loop(1, SEQ)
+        def _(k):
+            recv_o(k, h).wait_recv()
+
+        attn = jnp.concatenate([orecv[j, rows] for j in range(HEADS)], axis=1).astype(F32)
+        gated = (layer_norm(attn) * gate[rows, :].astype(F32)).astype(BF16)
+        layer_half = (dot(gated, wo[...]) + tokens[rows, :].astype(F32)).astype(BF16)
+        layer_out[rows, :] = layer_half
+        out = dot(layer_half, wp[...])
+        out_hat[rows, :] = (
+            out * lax.rsqrt(jnp.sum(out * out, axis=-1, keepdims=True) + UNIT_EPSILON)
+        ).astype(BF16)
+        out_t = jnp.transpose(out)
+        norm_t = jnp.sqrt(jnp.sum(out_t * out_t, axis=0, keepdims=True) + UNIT_EPSILON)
+        unit_t = out_t / norm_t
+        hat_t = unit_t.astype(BF16)
+        pos_half = pos_t[:, rows]
+        pos_dot = jnp.sum(hat_t.astype(F32) * pos_half, axis=0, keepdims=True) * (1.0 / WARMTH)
+        pos_logit = pos_dot + jnp.log(inverse_chance(pos_ids[:, rows].astype(F32)))
+        pos_exp = jnp.exp(pos_logit)
+
+        def scores(j, sums):
+            value = jnp.exp(dot(negs[j], hat_t) * (1.0 / WARMTH)) * cmask[j, :, rows]
+            kept[j] = value
+            return sums + jnp.sum(value, axis=0, keepdims=True)
+
+        total = lax.fori_loop(0, POOL, scores, pos_exp, unroll=8)
+        valid = s * ROWS + start + lax.broadcasted_iota(jnp.int32, (1, HALF), 1) < length
+        loss[:, rows] = jnp.where(valid, jnp.log(total) - pos_logit, 0.0)
+        share = jnp.where(valid, 1.0 / (total * HIST), 0.0)
+        pos_weight = jnp.where(valid, pos_exp / total - 1.0, 0.0) * (1.0 / HIST)
+
+        @pl.loop(0, POOL, unroll=4)
+        def _(j):
+            wt[pl.ds(pl.multiple_of(j * ROWS, ROWS), ROWS), rows] = (kept[j] * share).astype(BF16)
+
+        rows_t = dot(negs_t[...], wt[:, rows])
+        grad_t = (pos_weight * pos_half + rows_t) * (1.0 / WARMTH)
+        d_out[rows, :] = jnp.transpose(
+            (grad_t - unit_t * jnp.sum(unit_t * grad_t, axis=0, keepdims=True)) / norm_t
+        ).astype(BF16)
+
+    out_loss = pltpu.make_async_copy(loss, loss_ref, out_sem.at[3])
+    out_loss.start()
 
     half = WIDTH // 2
     mine = pl.ds(pl.multiple_of(core * half, half), half)
     theirs = pl.ds(pl.multiple_of((1 - core) * half, half), half)
-    pcs[...] = term[theirs, :].astype(BF16)
+    pcs[...] = dot_tn(layer_out[:, theirs], d_out[...]).astype(BF16)
     send_pc = remote(pcs, pcr, pc_sem.at[0], pc_sem.at[1], pool=sibling)
     send_pc.start()
+    term[...] = dot_tn(layer_out[:, mine], d_out[...])
 
     def place(n):
         y_at = (y + 1 + n // 2) % 4
@@ -453,40 +504,49 @@
 
     def portion(j):
         weight = wt[pl.ds(pl.multiple_of(j * ROWS, ROWS), ROWS), :]
-        return dot(weight, out_hat) * (1.0 / WARMTH)
-
-    @pl.loop(0, 8)
+        return dot(weight, out_hat[...]) * (1.0 / WARMTH)
+
+    @pl.loop(0, 4, unroll=2)
     def _(n):
         y_at, x_at = place(n)
         m = 2 * y_at + x_at
         cs[m] = portion(2 * m + 1 - core).astype(BF16)
         send_c(m).start()
 
-    def plane(q):
-        return {"batch": q // 8, "pool": 2 * (q % 8) + core}
-
-    def send_px(k):
-        q = (q_own + k) % GRID
+    x = 2 * b + xlo
+
+    def plane(n, sign):
+        dx, dy = STEPS[n]
+        x_at = (x + (dx if sign > 0 else 4 - dx)) % 4
+        y_at = (y + (dy if sign > 0 else 4 - dy)) % 4
+        q = (x_at // 2) * 8 + y_at * 2 + x_at % 2
+        return q, {"batch": x_at // 2, "pool": y_at * 4 + (x_at % 2) * 2 + core}
+
+    def send_px(n):
+        q, device = plane(n, 1)
         return remote(
             pxs.at[pl.ds(pl.multiple_of(q * 32, 32), 32), :],
             pxr.at[q_own],
-            px_sem.at[0, k],
-            px_sem.at[1, k],
-            **plane(q),
-        )
-
-    def recv_px(k):
-        q = (q_own + GRID - k) % GRID
-        return remote(
-            pxs.at[pl.ds(0, 32), :], pxr.at[q], px_sem.at[0, k], px_sem.at[1, k], **plane(q)
-        )
+            px_sem.at[0, n],
+            px_sem.at[1, n],
+            **device,
+        )
+
+    def recv_px(n):
+        q, device = plane(n, -1)
+        return remote(pxs.at[pl.ds(0, 32), :], pxr.at[q], px_sem.at[0, n], px_sem.at[1, n], **device)
 
     send_pc.wait_recv()
-    pxs[...] = (term[mine, :] + pcr[...].astype(F32)).astype(BF16)
-
-    @pl.loop(1, GRID)
-    def _(k):
-        send_px(k).start()
+    pxs[...] = (term[...] + pcr[...].astype(F32)).astype(BF16)
+    for n in range(GRID - 1):
+        send_px(n).start()
+
+    @pl.loop(4, 8, unroll=2)
+    def _(n):
+        y_at, x_at = place(n)
+        m = 2 * y_at + x_at
+        cs[m] = portion(2 * m + 1 - core).astype(BF16)
+        send_c(m).start()
 
     pxr[q_own] = pxs[pl.ds(pl.multiple_of(q_own * 32, 32), 32), :]
 
@@ -498,27 +558,30 @@
             ybs.at[k], ybr.at[k], yb_sem.at[0, k], yb_sem.at[1, k], pool=((y + k) % 4) * 4 + p % 4
         )
 
-    @pl.loop(0, 8)
+    @pl.loop(0, 4)
     def _(n):
-        y_at, x_at = place(n)
-        m = 2 * y_at + x_at
-        mixed = portion(2 * m + core)
-        send_c(m).wait_recv()
-        mixed = mixed + cr[m].astype(F32)
-        own[m] = mixed
-
-        @pl.when(n % 2 == 0)
+        y_at = (y + 1 + n) % 4
+        m_far = 2 * y_at + 1 - xlo
+        m_near = 2 * y_at + xlo
+        far = portion(2 * m_far + core)
+        near = portion(2 * m_near + core)
+        send_c(m_far).wait_recv()
+        far = far + cr[m_far].astype(F32)
+        xs[y_at] = far[:HALF].astype(BF16)
+        send_x(y_at).start()
+        send_c(m_near).wait_recv()
+        near = near + cr[m_near].astype(F32)
+        own[m_near] = near
+
+        @pl.when(n < 3)
         def _():
-            xs[y_at] = mixed[:128].astype(BF16)
-            send_x(y_at).start()
-
-        @pl.when(n < 6)
+            ybs[1 + n, 1 - xlo] = far[HALF:].astype(BF16)
+            ybs[1 + n, xlo] = near[HALF:].astype(BF16)
+            send_yb(1 + n).start()
+
+        @pl.when(n == 3)
         def _():
-            ybs[1 + n // 2, x_at] = mixed[128:].astype(BF16)
-
-        @pl.when((n < 6) & (n % 2 == 1))
-        def _():
-            send_yb(1 + n // 2).start()
+            own[m_far] = far
 
     def send_pz(k):
         return remote(pzr.at[s], pzr.at[s], pz_sem.at[0, k], pz_sem.at[1, k], seq=(s + k) % SEQ)
@@ -527,18 +590,17 @@
         src = (s + SEQ - k) % SEQ
         return remote(pzr.at[src], pzr.at[src], pz_sem.at[0, k], pz_sem.at[1, k], seq=src)
 
-    @pl.loop(1, GRID)
-    def _(k):
-        recv_px(k).wait_recv()
+    for n in range(GRID - 1):
+        recv_px(n).wait_recv()
 
     block = pxr[0].astype(F32)
     for q in range(1, GRID):
         block = block + pxr[q].astype(F32)
     pzr[s] = block.astype(BF16)
 
-    @pl.loop(1, SEQ)
-    def _(k):
-        send_pz(k).start()
+    @pl.loop(0, SEQ - 1)
+    def _(i):
+        send_pz(far_first(i)).start()
 
     def send_y(k):
         return remote(
@@ -575,87 +637,92 @@
         whole = whole + pzr[z].astype(F32)
     fin[core * GRID + q_own] = whole.astype(BF16)
 
-    def send_f(k):
+    def send_f(n):
         at = core * GRID + q_own
-        return remote(fin.at[at], fin.at[at], f_sem.at[0, k], f_sem.at[1, k], **plane((q_own + k) % GRID))
-
-    def recv_f(k):
-        q = (q_own + GRID - k) % GRID
+        return remote(fin.at[at], fin.at[at], f_sem.at[0, n], f_sem.at[1, n], **plane(n, 1)[1])
+
+    def recv_f(n):
+        q, device = plane(n, -1)
         at = core * GRID + q
-        return remote(fin.at[at], fin.at[at], f_sem.at[0, k], f_sem.at[1, k], **plane(q))
-
-    def send_fc(k):
-        at = core * GRID + (q_own + GRID - k) % GRID
-        return remote(fin.at[at], fin.at[at], fc_sem.at[0, k], fc_sem.at[1, k], pool=sibling)
-
-    def recv_fc(k):
-        at = (1 - core) * GRID + (q_own + GRID - k) % GRID
-        return remote(fin.at[at], fin.at[at], fc_sem.at[0, k], fc_sem.at[1, k], pool=sibling)
-
-    @pl.loop(1, GRID)
-    def _(k):
-        send_f(k).start()
-
-    send_fc(0).start()
-
-    def send_z(k):
-        return remote(zs.at[k], zr.at[k], z_sem.at[0, k], z_sem.at[1, k], seq=(s + k) % SEQ)
-
-    upper = own[2 * y + xlo, :128]
+        return remote(fin.at[at], fin.at[at], f_sem.at[0, n], f_sem.at[1, n], **device)
+
+    ours = fin.at[pl.ds(core * GRID, GRID)]
+    others = fin.at[pl.ds((1 - core) * GRID, GRID)]
+    send_fc = remote(ours, ours, fc_sem.at[0], fc_sem.at[1], pool=sibling)
+    recv_fc = remote(others, others, fc_sem.at[0], fc_sem.at[1], pool=sibling)
+    out_ours = pltpu.make_async_copy(ours, dproj_ref.at[pl.ds(core * GRID, GRID)], out_sem.at[0])
+    out_others = pltpu.make_async_copy(
+        others, dproj_ref.at[pl.ds((1 - core) * GRID, GRID)], out_sem.at[1]
+    )
+
+    for n in range(GRID - 1):
+        send_f(n).start()
+
+    def send_z(h, k):
+        return remote(
+            zs.at[h, k], zr.at[h, k], z_sem.at[h, 0, k], z_sem.at[h, 1, k], seq=(s + k) % SEQ
+        )
+
+    def project(h, neg_sum):
+        rows = slice(h * HALF, (h + 1) * HALF)
+        neg = neg_embed[rows, :].astype(F32)
+        neg_norm = jnp.sqrt(jnp.sum(neg * neg, axis=-1, keepdims=True) + UNIT_EPSILON)
+        unit = neg_unit[rows, :]
+        neg_t[:, rows] = jnp.transpose(
+            (neg_sum - unit * jnp.sum(unit * neg_sum, axis=-1, keepdims=True)) / neg_norm
+        )
+
+        @pl.loop(0, SEQ - 1)
+        def _(i):
+            k = far_first(i)
+            cols = pl.ds(pl.multiple_of(((s + k) % SEQ) * 32, 32), 32)
+            zs[h, k] = neg_t[cols, rows].astype(BF16)
+            send_z(h, k).start()
+
+    send_xb.wait_recv()
+    project(1, own[2 * y + xlo, HALF:] + xbr[...].astype(F32))
+    upper = own[2 * y + xlo, :HALF]
     for k in range(1, 4):
         send_y(k).wait_recv()
         upper = upper + yr[k].astype(F32)
-    send_xb.wait_recv()
-    lower = own[2 * y + xlo, 128:] + xbr[...].astype(F32)
-    neg_sum = jnp.concatenate([upper, lower], axis=0)
-    neg = neg_embed[...].astype(F32)
-    neg_norm = jnp.sqrt(jnp.sum(neg * neg, axis=-1, keepdims=True) + UNIT_EPSILON)
-    unit = neg_unit[...]
-    neg_t[...] = jnp.transpose(
-        (neg_sum - unit * jnp.sum(unit * neg_sum, axis=-1, keepdims=True)) / neg_norm
-    )
-
-    @pl.loop(1, SEQ)
-    def _(k):
-        rows = pl.ds(pl.multiple_of(((s + k) % SEQ) * 32, 32), 32)
-        zs[k] = neg_t[rows, :].astype(BF16)
-        send_z(k).start()
-
-    @pl.loop(1, GRID)
-    def _(k):
-        recv_f(k).wait_recv()
-        send_fc(k).start()
-
-    part = neg_t[pl.ds(pl.multiple_of(s * 32, 32), 32), :]
-    for k in range(1, SEQ):
-        send_z(k).wait_recv()
-        part = part + zr[k].astype(F32)
-    dneg_ref[...] = part
-
-    @pl.loop(0, GRID)
-    def _(k):
-        recv_fc(k).wait_recv()
-
-    dproj_ref[...] = fin[...]
+    project(0, upper)
+
+    for n in range(GRID - 1):
+        recv_f(n).wait_recv()
+    send_fc.start()
+    out_ours.start()
+
+    for h in (1, 0):
+        rows = slice(h * HALF, (h + 1) * HALF)
+        part = neg_t[pl.ds(pl.multiple_of(s * 32, 32), 32), rows]
+        for k in range(1, SEQ):
+            send_z(h, k).wait_recv()
+            part = part + zr[h, k].astype(F32)
+        dneg[:, rows] = part
+    out_dneg = pltpu.make_async_copy(dneg, dneg_ref, out_sem.at[2])
+    out_dneg.start()
+
+    recv_fc.wait_recv()
+    out_others.start()
 
     @pl.loop(1, SEQ)
     def _(k):
         send_kv(k).wait_send()
         send_q(k).wait_send()
-        send_o(k).wait_send()
+        send_o(k, 0).wait_send()
+        send_o(k, 1).wait_send()
         send_pz(k).wait_send()
-        send_z(k).wait_send()
+        send_z(0, k).wait_send()
+        send_z(1, k).wait_send()
 
     @pl.loop(1, POOL)
     def _(k):
         send_ids(k).wait_send()
         send_negs(k).wait_send()
-        send_px(k).wait_send()
-        send_f(k).wait_send()
-
-    @pl.loop(0, GRID)
-    def _(k):
-        send_fc(k).wait_send()
+
+    for n in range(GRID - 1):
+        send_px(n).wait_send()
+        send_f(n).wait_send()
 
     @pl.loop(0, 8)
     def _(m):
@@ -672,6 +739,11 @@
 
     send_xb.wait_send()
     send_pc.wait_send()
+    send_fc.wait_send()
+    out_loss.wait()
+    out_dneg.wait()
+    out_ours.wait()
+    out_others.wait()
 
 
 def finish(loss, dneg_t, dproj, loss_out, dneg_out, dproj_out):
@@ -683,7 +755,6 @@
 def body(tokens, w_in, w_out, w_proj, pos_embed, pos_ids, lengths, neg_embed, neg_ids):
     vmem = pl.BlockSpec(memory_space=pltpu.VMEM)
     hbm = pl.BlockSpec(memory_space=pl.ANY)
-    smem = pl.BlockSpec(memory_space=pltpu.SMEM)
     dma = pltpu.SemaphoreType.DMA
     loss, dneg_t, dproj = pl.pallas_call(
         kernel,
@@ -692,12 +763,15 @@
             jax.ShapeDtypeStruct((EMBED // SEQ, ROWS), F32),
             jax.ShapeDtypeStruct((2 * GRID, 32, EMBED), BF16),
         ),
-        in_specs=[hbm, hbm, hbm, hbm, hbm, vmem, smem, hbm, vmem],
-        out_specs=(vmem, vmem, vmem),
+        in_specs=[hbm] * 9,
+        out_specs=(hbm, hbm, hbm),
         scratch_shapes=[
             pltpu.VMEM((ROWS, WIDTH), BF16),
             pltpu.VMEM((ROWS, EMBED), BF16),
             pltpu.VMEM((ROWS, EMBED), BF16),
+            pltpu.VMEM((1, ROWS), jnp.int32),
+            pltpu.VMEM((1, ROWS), jnp.int32),
+            pltpu.SMEM((1,), jnp.int32),
             pltpu.VMEM((8, WIDTH, 256), BF16),
             pltpu.VMEM((4, WIDTH, 256), BF16),
             pltpu.VMEM((WIDTH, WIDTH), BF16),
@@ -715,8 +789,11 @@
             pltpu.VMEM((EMBED, POOL * ROWS), BF16),
             pltpu.VMEM((POOL, 1, ROWS), jnp.int32),
             pltpu.VMEM((POOL, ROWS, ROWS), F32),
-            pltpu.VMEM((POOL, ROWS, ROWS), F32),
+            pltpu.VMEM((POOL, ROWS, HALF), F32),
             pltpu.VMEM((POOL * ROWS, ROWS), BF16),
+            pltpu.VMEM((ROWS, WIDTH), BF16),
+            pltpu.VMEM((ROWS, EMBED), BF16),
+            pltpu.VMEM((ROWS, EMBED), BF16),
             pltpu.VMEM((EMBED, ROWS), F32),
             pltpu.VMEM((ROWS, EMBED), F32),
             pltpu.VMEM((8, ROWS, EMBED), BF16),
@@ -731,19 +808,21 @@
             pltpu.VMEM((128, EMBED), BF16),
             pltpu.VMEM((128, EMBED), BF16),
             pltpu.VMEM((EMBED, ROWS), F32),
-            pltpu.VMEM((SEQ, 32, ROWS), BF16),
-            pltpu.VMEM((SEQ, 32, ROWS), BF16),
-            pltpu.VMEM((WIDTH, EMBED), F32),
+            pltpu.VMEM((2, SEQ, 32, HALF), BF16),
+            pltpu.VMEM((2, SEQ, 32, HALF), BF16),
+            pltpu.VMEM((WIDTH // 2, EMBED), F32),
             pltpu.VMEM((WIDTH // 2, EMBED), BF16),
             pltpu.VMEM((WIDTH // 2, EMBED), BF16),
             pltpu.VMEM((WIDTH // 2, EMBED), BF16),
             pltpu.VMEM((GRID, 32, EMBED), BF16),
             pltpu.VMEM((SEQ, 32, EMBED), BF16),
             pltpu.VMEM((2 * GRID, 32, EMBED), BF16),
-            dma((30,)),
+            pltpu.VMEM((1, ROWS), F32),
+            pltpu.VMEM((EMBED // SEQ, ROWS), F32),
+            dma((33,)),
             dma((2, SEQ)),
             dma((2, SEQ)),
-            dma((2, SEQ)),
+            dma((2, 2, SEQ)),
             dma((2, POOL)),
             dma((2, POOL)),
             dma((2, 8)),
@@ -751,12 +830,13 @@
             dma((2, 4)),
             dma((2, 4)),
             dma((2,)),
-            dma((2, SEQ)),
+            dma((2, 2, SEQ)),
             dma((2,)),
             dma((2, GRID)),
             dma((2, SEQ)),
             dma((2, GRID)),
-            dma((2, GRID)),
+            dma((2,)),
+            dma((4,)),
         ],
         compiler_params=pltpu.CompilerParams(
             collective_id=0, has_side_effects=True, vmem_limit_bytes=56 * 1024 * 1024

time: 95.9 us -> 90.7 us (0.946)
  Pallas kernels: 94.5 us -> 89.3 us
    pallas_call x1, Pallas kernels: 92.4 us -> 87.2 us  [body(): pl.pallas_call(kernel, out_shape=(jax.ShapeDtypeStruct((1, ROWS), F32), j...]
where the time goes in v3:
time: 90.7 us; the launch traced here: 90.6 us
  Pallas kernels  89.3 us (98%)
  between operations  1.29 us (1%)
    pallas_call x1, Pallas kernels, body(): pl.pallas_call(kernel, out_shape=(jax.ShapeDtypeStruct((1, ROWS), F32), j...  87.2 us
    pallas_call x1, Pallas kernels, body(): pl.pallas_call(finish, out_shape=(jax.ShapeDtypeStruct((1, ROWS), F32), j...  2.11 us

profile of v3, /device:TPU:1, one launch (start us, length us, event | category | flops | bytes accessed | tf_op | source)
XLA Modules:
  0.0 90.6 jit_solution(11358895332673235402)
XLA Ops:
  1.3 87.2 %shard_map.112 = (f32[1,256]{1,0:T(1,128)}, f32[32,256]{1,0:T(8,128)}, bf16[32,32,256]{2,1,0:T(8,128)(2,1)}) custom-call(bf16[256,1024]{1,0:T(8,128)(2,1)} %bitcast.7, bf16[1024,4096]{1,0:T(8,128)(2,1)} %w_in.1, bf16[1024,1024]{1,0:T(8,128)(2,1)} %w_out.1, bf16[1024,256]{1,0:T(8,128)(2,1)} %w_proj.1, bf16[256,256]{1,0:T(8,128)(2,1)} %bitcast.9, ...), custom_call_target="tpu_custom_call" | custom-call | tf_op jit(solution)/shard_map/pallas_call | solution.py:759
  88.5 2.1 %shard_map.113 = (f32[1,256]{1,0:T(1,128)}, f32[32,256]{1,0:T(8,128)}, f32[1024,256]{1,0:T(8,128)}) custom-call(f32[1,256]{1,0:T(1,128)} %get-tuple-element.9.loss, f32[32,256]{1,0:T(8,128)} %get-tuple-element.10.dneg_t, bf16[1024,256]{1,0:T(8,128)(2,1)} %bitcast.8), custom_call_target="tpu_custom_call" | custom-call | tf_op jit(solution)/shard_map/pallas_call | solution.py:855

commit v4 on v3

--- a/solution.py
+++ b/solution.py
@@ -424,6 +424,16 @@
     def _(i):
         send_o(far_first(i - 1), 1).start()
 
+    @pl.loop(1, SEQ)
+    def _(k):
+        send_kv(k).wait_send()
+        send_q(k).wait_send()
+
+    @pl.loop(1, POOL)
+    def _(k):
+        send_ids(k).wait_send()
+        send_negs(k).wait_send()
+
     @pl.loop(0, POOL)
     def _(k):
         @pl.when(k > 0)
@@ -602,6 +612,19 @@
     def _(i):
         send_pz(far_first(i)).start()
 
+    @pl.loop(1, SEQ)
+    def _(k):
+        send_o(k, 0).wait_send()
+        send_o(k, 1).wait_send()
+
+    @pl.loop(0, 8)
+    def _(m):
+        send_c(m).wait_send()
+
+    send_pc.wait_send()
+    for n in range(GRID - 1):
+        send_px(n).wait_send()
+
     def send_y(k):
         return remote(
             ys.at[k], yr.at[k], y_sem.at[0, k], y_sem.at[1, k], pool=((y + k) % 4) * 4 + p % 4
@@ -628,6 +651,14 @@
     own[2 * y + xlo, :128] = own[2 * y + xlo, :128] + xr[y].astype(F32)
     own[2 * y + xlo, 128:] = lower
 
+    @pl.loop(0, 4)
+    def _(i):
+        send_x(i).wait_send()
+
+    @pl.loop(1, 4)
+    def _(k):
+        send_yb(k).wait_send()
+
     @pl.loop(1, SEQ)
     def _(k):
         recv_pz(k).wait_recv()
@@ -687,10 +718,22 @@
         upper = upper + yr[k].astype(F32)
     project(0, upper)
 
+    @pl.loop(1, SEQ)
+    def _(k):
+        send_pz(k).wait_send()
+
+    @pl.loop(1, 4)
+    def _(k):
+        send_y(k).wait_send()
+
+    send_xb.wait_send()
+
     for n in range(GRID - 1):
         recv_f(n).wait_recv()
     send_fc.start()
     out_ours.start()
+    for n in range(GRID - 1):
+        send_f(n).wait_send()
 
     for h in (1, 0):
         rows = slice(h * HALF, (h + 1) * HALF)
@@ -707,38 +750,9 @@
 
     @pl.loop(1, SEQ)
     def _(k):
-        send_kv(k).wait_send()
-        send_q(k).wait_send()
-        send_o(k, 0).wait_send()
-        send_o(k, 1).wait_send()
-        send_pz(k).wait_send()
         send_z(0, k).wait_send()
         send_z(1, k).wait_send()
 
-    @pl.loop(1, POOL)
-    def _(k):
-        send_ids(k).wait_send()
-        send_negs(k).wait_send()
-
-    for n in range(GRID - 1):
-        send_px(n).wait_send()
-        send_f(n).wait_send()
-
-    @pl.loop(0, 8)
-    def _(m):
-        send_c(m).wait_send()
-
-    @pl.loop(0, 4)
-    def _(i):
-        send_x(i).wait_send()
-
-    @pl.loop(1, 4)
-    def _(k):
-        send_y(k).wait_send()
-        send_yb(k).wait_send()
-
-    send_xb.wait_send()
-    send_pc.wait_send()
     send_fc.wait_send()
     out_loss.wait()
     out_dneg.wait()

time: 90.7 us -> 90.7 us (level)
  no operation moved by 1% of the time
where the time goes in v4:
time: 90.7 us; the launch traced here: 90.6 us
  Pallas kernels  89.3 us (98%)
  between operations  1.29 us (1%)
    pallas_call x1, Pallas kernels, body(): pl.pallas_call(kernel, out_shape=(jax.ShapeDtypeStruct((1, ROWS), F32), j...  87.2 us
    pallas_call x1, Pallas kernels, body(): pl.pallas_call(finish, out_shape=(jax.ShapeDtypeStruct((1, ROWS), F32), j...  2.11 us

profile of v4, /device:TPU:1, one launch (start us, length us, event | category | flops | bytes accessed | tf_op | source)
XLA Modules:
  0.0 90.6 jit_solution(12355425926216444716)
XLA Ops:
  1.3 87.2 %shard_map.112 = (f32[1,256]{1,0:T(1,128)}, f32[32,256]{1,0:T(8,128)}, bf16[32,32,256]{2,1,0:T(8,128)(2,1)}) custom-call(bf16[256,1024]{1,0:T(8,128)(2,1)} %bitcast.7, bf16[1024,4096]{1,0:T(8,128)(2,1)} %w_in.1, bf16[1024,1024]{1,0:T(8,128)(2,1)} %w_out.1, bf16[1024,256]{1,0:T(8,128)(2,1)} %w_proj.1, bf16[256,256]{1,0:T(8,128)(2,1)} %bitcast.9, ...), custom_call_target="tpu_custom_call" | custom-call | tf_op jit(solution)/shard_map/pallas_call | solution.py:773
  88.5 2.1 %shard_map.113 = (f32[1,256]{1,0:T(1,128)}, f32[32,256]{1,0:T(8,128)}, f32[1024,256]{1,0:T(8,128)}) custom-call(f32[1,256]{1,0:T(1,128)} %get-tuple-element.9.loss, f32[32,256]{1,0:T(8,128)} %get-tuple-element.10.dneg_t, bf16[1024,256]{1,0:T(8,128)(2,1)} %bitcast.8), custom_call_target="tpu_custom_call" | custom-call | tf_op jit(solution)/shard_map/pallas_call | solution.py:869

commit v5 on v4

--- a/solution.py
+++ b/solution.py
@@ -67,6 +67,10 @@
 
 def far_first(i):
     return 4 + (1 - 2 * (i % 2)) * ((i + 1) // 2)
+
+
+def near_first(i):
+    return far_first((14 - i) % 8)
 
 
 def remote(src, dst, send, recv, **device):
@@ -221,10 +225,10 @@
         )
 
     load_t.start()
-    for c in load_kv(4) + load_ids:
+    for c in load_kv(7) + load_ids:
         c.start()
     for i in range(1, 8):
-        for c in load_kv(far_first(i)):
+        for c in load_kv(near_first(i)):
             c.start()
     for i in range(4):
         load_q(i, 0).start()
@@ -257,13 +261,13 @@
         kvs[k, 0] = both[:, :HEAD].astype(BF16)
         kvs[k, 1] = jnp.where(row_valid, both[:, HEAD:], 0.0).astype(BF16)
 
-    make_kv(4)
+    make_kv(7)
     pl.semaphore_wait(barrier, (SEQ - 1) + (POOL - 1) + POOL // 2)
-    send_kv(4).start()
+    send_kv(7).start()
 
     @pl.loop(1, SEQ)
     def _(i):
-        k = far_first(i)
+        k = near_first(i)
         make_kv(k)
 
         @pl.when(i < SEQ - 1)
@@ -760,14 +764,32 @@
     out_others.wait()
 
 
-def finish(loss, dneg_t, dproj, loss_out, dneg_out, dproj_out):
-    loss_out[...] = loss[...]
-    dneg_out[...] = dneg_t[...]
-    dproj_out[...] = dproj[...].astype(F32)
+def finish(loss, dneg_t, dproj, loss_out, dneg_out, dproj_out, narrow, wide, sem):
+    rows = WIDTH // 4
+    loss_copy = pltpu.make_async_copy(loss, loss_out, sem.at[8])
+    dneg_copy = pltpu.make_async_copy(dneg_t, dneg_out, sem.at[9])
+    loads = [
+        pltpu.make_async_copy(dproj.at[pl.ds(c * rows, rows)], narrow.at[c], sem.at[c]) for c in range(4)
+    ]
+    stores = [
+        pltpu.make_async_copy(wide.at[c], dproj_out.at[pl.ds(c * rows, rows)], sem.at[4 + c])
+        for c in range(4)
+    ]
+    for load in loads:
+        load.start()
+    loss_copy.start()
+    dneg_copy.start()
+    for c in range(4):
+        loads[c].wait()
+        wide[c] = narrow[c].astype(F32)
+        stores[c].start()
+    for store in stores:
+        store.wait()
+    loss_copy.wait()
+    dneg_copy.wait()
 
 
 def body(tokens, w_in, w_out, w_proj, pos_embed, pos_ids, lengths, neg_embed, neg_ids):
-    vmem = pl.BlockSpec(memory_space=pltpu.VMEM)
     hbm = pl.BlockSpec(memory_space=pl.ANY)
     dma = pltpu.SemaphoreType.DMA
     loss, dneg_t, dproj = pl.pallas_call(
@@ -873,8 +895,13 @@
             jax.ShapeDtypeStruct((EMBED // SEQ, ROWS), F32),
             jax.ShapeDtypeStruct((WIDTH, EMBED), F32),
         ),
-        in_specs=[vmem, vmem, vmem],
-        out_specs=(vmem, vmem, vmem),
+        in_specs=[hbm] * 3,
+        out_specs=(hbm, hbm, hbm),
+        scratch_shapes=[
+            pltpu.VMEM((4, WIDTH // 4, EMBED), BF16),
+            pltpu.VMEM((4, WIDTH // 4, EMBED), F32),
+            dma((10,)),
+        ],
     )(loss, dneg_t, dproj.reshape(WIDTH, EMBED))
     return (loss, jnp.transpose(dneg_t)[None], dproj)
 

time: 90.7 us -> 90.4 us (level)
  no operation moved by 1% of the time
where the time goes in v5:
time: 90.4 us; the launch traced here: 90.3 us
  Pallas kernels  89 us (98%)
  between operations  1.29 us (1%)
    pallas_call x1, Pallas kernels, body(): pl.pallas_call(kernel, out_shape=(jax.ShapeDtypeStruct((1, ROWS), F32), j...  86.8 us
    pallas_call x1, Pallas kernels, body(): pl.pallas_call(finish, out_shape=(jax.ShapeDtypeStruct((1, ROWS), F32), j...  2.22 us

profile of v5, /device:TPU:1, one launch (start us, length us, event | category | flops | bytes accessed | tf_op | source)
XLA Modules:
  0.0 90.3 jit_solution(12708520509949470128)
XLA Ops:
  1.3 86.8 %shard_map.112 = (f32[1,256]{1,0:T(1,128)}, f32[32,256]{1,0:T(8,128)}, bf16[32,32,256]{2,1,0:T(8,128)(2,1)}) custom-call(bf16[256,1024]{1,0:T(8,128)(2,1)} %bitcast.7, bf16[1024,4096]{1,0:T(8,128)(2,1)} %w_in.1, bf16[1024,1024]{1,0:T(8,128)(2,1)} %w_out.1, bf16[1024,256]{1,0:T(8,128)(2,1)} %w_proj.1, bf16[256,256]{1,0:T(8,128)(2,1)} %bitcast.9, ...), custom_call_target="tpu_custom_call" | custom-call | tf_op jit(solution)/shard_map/pallas_call | solution.py:795
  88.1 2.2 %shard_map.113 = (f32[1,256]{1,0:T(1,128)}, f32[32,256]{1,0:T(8,128)}, f32[1024,256]{1,0:T(8,128)}) custom-call(f32[1,256]{1,0:T(1,128)} %get-tuple-element.9.loss, f32[32,256]{1,0:T(8,128)} %get-tuple-element.10.dneg_t, bf16[1024,256]{1,0:T(8,128)(2,1)} %bitcast.8), custom_call_target="tpu_custom_call" | custom-call | tf_op jit(solution)/shard_map/pallas_call | solution.py:891

commit v6 on v5

--- a/solution.py
+++ b/solution.py
@@ -67,6 +67,10 @@
 
 def far_first(i):
     return 4 + (1 - 2 * (i % 2)) * ((i + 1) // 2)
+
+
+def far_y(n):
+    return 2 + (1 - 2 * (n % 2)) * ((n + 1) // 2)
 
 
 def near_first(i):
@@ -509,7 +513,7 @@
     term[...] = dot_tn(layer_out[:, mine], d_out[...])
 
     def place(n):
-        y_at = (y + 1 + n // 2) % 4
+        y_at = (y + far_y(n // 2)) % 4
         x_at = xlo + (1 - n % 2) * (1 - 2 * xlo)
         return y_at, x_at
 
@@ -574,7 +578,8 @@
 
     @pl.loop(0, 4)
     def _(n):
-        y_at = (y + 1 + n) % 4
+        k = far_y(n)
+        y_at = (y + k) % 4
         m_far = 2 * y_at + 1 - xlo
         m_near = 2 * y_at + xlo
         far = portion(2 * m_far + core)
@@ -589,9 +594,9 @@
 
         @pl.when(n < 3)
         def _():
-            ybs[1 + n, 1 - xlo] = far[HALF:].astype(BF16)
-            ybs[1 + n, xlo] = near[HALF:].astype(BF16)
-            send_yb(1 + n).start()
+            ybs[k, 1 - xlo] = far[HALF:].astype(BF16)
+            ybs[k, xlo] = near[HALF:].astype(BF16)
+            send_yb(k).start()
 
         @pl.when(n == 3)
         def _():
@@ -636,8 +641,9 @@
 
     send_xb = remote(xbs, xbr, xb_sem.at[0], xb_sem.at[1], pool=across)
 
-    @pl.loop(1, 4)
-    def _(k):
+    @pl.loop(0, 3)
+    def _(n):
+        k = far_y(n)
         i = (y + k) % 4
         send_x(i).wait_recv()
         ys[k] = (own[2 * i + xlo, :128] + xr[i].astype(F32)).astype(BF16)

time: 90.4 us -> 90.2 us (level)
  no operation moved by 1% of the time
where the time goes in v6:
time: 90.2 us; the launch traced here: 90.1 us
  Pallas kernels  88.8 us (98%)
  between operations  1.29 us (1%)
    pallas_call x1, Pallas kernels, body(): pl.pallas_call(kernel, out_shape=(jax.ShapeDtypeStruct((1, ROWS), F32), j...  86.6 us
    pallas_call x1, Pallas kernels, body(): pl.pallas_call(finish, out_shape=(jax.ShapeDtypeStruct((1, ROWS), F32), j...  2.22 us

profile of v6, /device:TPU:1, one launch (start us, length us, event | category | flops | bytes accessed | tf_op | source)
XLA Modules:
  0.0 90.1 jit_solution(5692417144999971198)
XLA Ops:
  1.3 86.6 %shard_map.112 = (f32[1,256]{1,0:T(1,128)}, f32[32,256]{1,0:T(8,128)}, bf16[32,32,256]{2,1,0:T(8,128)(2,1)}) custom-call(bf16[256,1024]{1,0:T(8,128)(2,1)} %bitcast.7, bf16[1024,4096]{1,0:T(8,128)(2,1)} %w_in.1, bf16[1024,1024]{1,0:T(8,128)(2,1)} %w_out.1, bf16[1024,256]{1,0:T(8,128)(2,1)} %w_proj.1, bf16[256,256]{1,0:T(8,128)(2,1)} %bitcast.9, ...), custom_call_target="tpu_custom_call" | custom-call | tf_op jit(solution)/shard_map/pallas_call | solution.py:801
  87.9 2.2 %shard_map.113 = (f32[1,256]{1,0:T(1,128)}, f32[32,256]{1,0:T(8,128)}, f32[1024,256]{1,0:T(8,128)}) custom-call(f32[1,256]{1,0:T(1,128)} %get-tuple-element.9.loss, f32[32,256]{1,0:T(8,128)} %get-tuple-element.10.dneg_t, bf16[1024,256]{1,0:T(8,128)(2,1)} %bitcast.8), custom_call_target="tpu_custom_call" | custom-call | tf_op jit(solution)/shard_map/pallas_call | solution.py:897
